TPU v7x, 32 devices: a whole 2x2x4 slice. The times are simulated.
32 devices in a mesh: seq: 16 (over z, x, core), chan: 2 (over y).
Axes of the slice: x: 2, y: 2, z: 4, core: 2. Of those that a mesh axis runs over, the one named last changes fastest.
Arguments:
- q_gate: float32 [8192, 2048], P('seq', 'chan'), may hold values from -6 to 6
- k_gate: float32 [8192, 2048], P('seq', 'chan'), may hold values from -6 to 6
- values: float32 [8192, 2048], P('seq', 'chan'), may hold values from -6 to 6
- filter_raw: float32 [8192, 128], P('seq'), may hold values from -6 to 6
- grad_out: float32 [8192, 2048], P('seq', 'chan'), may hold values from -6 to 6
Outputs:
- grad_q: float32 [8192, 2048], P('seq', 'chan')
- grad_k: float32 [8192, 2048], P('seq', 'chan')
- grad_v: float32 [8192, 2048], P('seq', 'chan')
- grad_filter: float32 [8192, 128], P('seq')
All inputs are finite; a program needn't handle non-finite values.
Results may differ from a plain program's by a relative error of at most 0.0001.
Values sent between devices are 32-bit elements; how exact they have to be, the bound alone decides.
A program may use at most 128 MiB of HBM per device.

v0:
```python
import jax
import jax.numpy as jnp
import numpy as np
from jax import lax
from jax.experimental import pallas as pl
from jax.experimental.pallas import tpu as pltpu
from jax.sharding import PartitionSpec as P

FINE = 128


def mul(form, left, right):
    return jnp.einsum(form, left, right, precision=lax.Precision.HIGH)


def tables(length):
    n1 = length // FINE
    k = np.arange(n1) + 0.25
    coarse = 2.0 * np.pi * np.outer(k, np.arange(n1)) / n1
    first = np.stack([np.cos(coarse), -np.sin(coarse)])
    last = np.stack([np.cos(coarse), -np.sin(coarse)]) / length
    twist = 2.0 * np.pi * np.outer(k, np.arange(FINE)) / length
    fine = 2.0 * np.pi * (np.outer(np.arange(FINE), np.arange(FINE)) % FINE) / FINE
    cos, sin = np.cos(fine), np.sin(fine)
    ahead = np.stack([np.stack([cos, sin]), np.stack([-sin, cos])])
    back = np.stack([np.stack([cos, -sin]), np.stack([sin, cos])])
    return [np.asarray(t, np.float32) for t in (first, last, np.cos(twist), np.sin(twist), ahead, back)]


def halves(table):
    high = table.astype(jnp.bfloat16)
    return high, (table - high.astype(np.float32)).astype(jnp.bfloat16)


def split_value(x):
    high = x.astype(jnp.bfloat16)
    return high, (x - high.astype(jnp.float32)).astype(jnp.bfloat16)


def dot(left, right):
    return jnp.dot(left, right, preferred_element_type=jnp.float32)


def kernel_tables(length):
    n1 = length // FINE
    k = np.arange(n1) + 0.25
    pos = np.arange(n1)[None, :] * FINE + np.arange(FINE)[:, None]
    angle = 2.0 * np.pi * (k[None, :, None] * pos[:, None, :]) / length
    ahead = np.concatenate([np.cos(angle), -np.sin(angle)], axis=1).astype(np.float32)
    back = np.swapaxes(ahead, 1, 2) / np.float32(length)
    ah, al = halves(ahead)
    bh, bl = halves(back)
    first = np.concatenate([ah, al, ah], axis=2)
    last = np.concatenate([bh, bl, bh], axis=2)
    fine = 2.0 * np.pi * (np.outer(np.arange(FINE), np.arange(FINE)) % FINE) / FINE
    cos, sin = np.cos(fine), np.sin(fine)
    fwd = np.block([[cos, sin], [-sin, cos]]).astype(np.float32)
    inv = np.block([[cos, -sin], [sin, cos]]).astype(np.float32)
    return first, last, np.stack(halves(fwd) + halves(inv))


def fold_tables(own, chans):
    spots = FINE // own
    lane = np.arange(FINE)
    spread = np.zeros((spots, FINE, FINE), np.float32)
    fold = np.zeros((spots, FINE, FINE), np.float32)
    for j in range(spots):
        spread[j, own * j + lane % own, lane] = 1.0
        used = lane[:chans]
        fold[j, used, own * j + used % own] = 1.0
    return spread.astype(jnp.bfloat16), fold.astype(jnp.bfloat16)


def order_table(width, nfilt, own):
    repeats, shards = width // nfilt, nfilt // own
    cols = np.arange(width).reshape(repeats, shards, own).transpose(1, 0, 2).reshape(-1)
    table = np.zeros((width, width), np.float32)
    table[cols, np.arange(width)] = 1.0
    return table.astype(jnp.bfloat16)


def low_lanes(rows):
    return lax.broadcasted_iota(jnp.int32, (rows, FINE), 1) < FINE // 2


def pack_kernel(k_ref, v_ref, o_ref, q_ref, table_ref, out_ref):
    table = table_ref[...]
    low = low_lanes(k_ref.shape[0])
    moved = []
    for block in (k_ref[...] * v_ref[...], o_ref[...] * q_ref[...]):
        high, rest = split_value(block)
        moved.append(dot(high, table) + dot(rest, table))
    for j in range(out_ref.shape[0] // 2):
        g, q = (m[:, FINE * j : FINE * (j + 1)] for m in moved)
        out_ref[2 * j] = jnp.where(low, g, pltpu.roll(q, FINE // 2, 1))
        out_ref[2 * j + 1] = jnp.where(low, pltpu.roll(g, FINE // 2, 1), q)


def unpack_kernel(in_ref, k_ref, v_ref, o_ref, table_ref, gq_ref, gk_ref, gv_ref):
    table = table_ref[...]
    low = low_lanes(k_ref.shape[0])
    conv, adj = [], []
    for j in range(in_ref.shape[0] // 2):
        a, b = in_ref[2 * j], in_ref[2 * j + 1]
        conv.append(jnp.where(low, a, pltpu.roll(b, FINE // 2, 1)))
        adj.append(jnp.where(low, pltpu.roll(a, FINE // 2, 1), b))
    moved = []
    for parts in (conv, adj):
        high, rest = split_value(jnp.concatenate(parts, axis=1))
        moved.append(dot(high, table) + dot(rest, table))
    gq_ref[...] = o_ref[...] * moved[0]
    gk_ref[...] = moved[1] * v_ref[...]
    gv_ref[...] = moved[1] * k_ref[...]


def spectral_kernel(
    pair_ref, filt_ref, first_ref, last_ref, fine_ref, spread_ref, fold_ref,
    out_ref, lags_ref, wide_ref, spec_a, spec_b,
):
    length = pair_ref.shape[0]
    n1 = length // FINE
    spots = spread_ref.shape[0]
    short = length // spots

    fh, fl = split_value(filt_ref[...])
    for j in range(spots):
        e = spread_ref[j]
        wide_ref[pl.ds(j, short, stride=spots), :] = dot(fh, e) + dot(fl, e)

    def ahead(n2, carry):
        x = jnp.concatenate(
            [r[pl.ds(n2, n1, stride=FINE), :] for r in (pair_ref, wide_ref)], axis=1
        )
        high, rest = split_value(x)
        y = dot(first_ref[n2], jnp.concatenate([high, high, rest], axis=0))
        spec_a[pl.ds(n2, 2 * n1, stride=FINE), :] = y[:, :FINE]
        spec_b[pl.ds(n2, 2 * n1, stride=FINE), :] = y[:, FINE:]
        return carry

    lax.fori_loop(0, FINE, ahead, 0, unroll=4)

    sign = jnp.where(low_lanes(FINE), 1.0, -1.0)

    def fine(which, re, im):
        high, rest = split_value(jnp.concatenate([re, im], axis=0))
        top, bottom = fine_ref[2 * which], fine_ref[2 * which + 1]
        return dot(top, high) + (dot(bottom, high) + dot(top, rest))

    def middle(k1, carry):
        at_re = pl.ds(pl.multiple_of(k1 * FINE, FINE), FINE)
        at_im = pl.ds(pl.multiple_of((k1 + n1) * FINE, FINE), FINE)
        z = fine(
            0,
            jnp.concatenate([spec_a[at_re, :], spec_b[at_re, :]], axis=1),
            jnp.concatenate([spec_a[at_im, :], spec_b[at_im, :]], axis=1),
        )
        pr, fr = z[:FINE, :FINE], z[:FINE, FINE:]
        pi, fi = z[FINE:, :FINE], z[FINE:, FINE:] * sign
        qr, qi = pltpu.roll(pr, FINE // 2, 1), pltpu.roll(pi, FINE // 2, 1)
        re = jnp.concatenate([fr * pr - fi * pi, pr * qr + pi * qi], axis=1)
        im = jnp.concatenate([fr * pi + fi * pr, pr * qi - pi * qr], axis=1)
        w = fine(1, re, im)
        spec_a[at_re, :] = w[:FINE, :FINE]
        spec_b[at_re, :] = w[:FINE, FINE:]
        spec_a[at_im, :] = w[FINE:, :FINE]
        spec_b[at_im, :] = w[FINE:, FINE:]
        return carry

    lax.fori_loop(0, n1, middle, 0, unroll=2)

    def behind(n2, carry):
        x = jnp.concatenate(
            [r[pl.ds(n2, 2 * n1, stride=FINE), :] for r in (spec_a, spec_b)], axis=1
        )
        high, rest = split_value(x)
        y = dot(last_ref[n2], jnp.concatenate([high, high, rest], axis=0))
        out_ref[pl.ds(n2, n1, stride=FINE), :] = y[:, :FINE]
        wide_ref[pl.ds(n2, n1, stride=FINE), :] = y[:, FINE:]
        return carry

    lax.fori_loop(0, FINE, behind, 0, unroll=4)

    total = jnp.zeros((short, FINE), jnp.float32)
    for j in range(spots):
        high, rest = split_value(wide_ref[pl.ds(j, short, stride=spots), :])
        total += dot(high, fold_ref[j]) + dot(rest, fold_ref[j])
    lags_ref[...] = total


VMEM_BYTES = 60 << 20


def pack(k_gate, values, grad_out, q_gate, shards, table):
    rows, width = k_gate.shape
    tile = 128
    block = pl.BlockSpec((tile, width), lambda i: (i, 0))
    return pl.pallas_call(
        pack_kernel,
        grid=(rows // tile,),
        in_specs=[block] * 4 + [pl.BlockSpec((width, width), lambda i: (0, 0))],
        out_specs=pl.BlockSpec((shards, tile, FINE), lambda i: (0, i, 0)),
        out_shape=jax.ShapeDtypeStruct((shards, rows, FINE), jnp.float32),
        compiler_params=pltpu.CompilerParams(vmem_limit_bytes=VMEM_BYTES),
        cost_estimate=pl.CostEstimate(
            flops=8 * rows * width * width, bytes_accessed=24 * rows * width, transcendentals=0
        ),
        name="pack",
    )(k_gate, values, grad_out, q_gate, table)


def unpack(back, k_gate, values, grad_out, table):
    rows, width = k_gate.shape
    tile = 128
    block = pl.BlockSpec((tile, width), lambda i: (i, 0))
    return pl.pallas_call(
        unpack_kernel,
        grid=(rows // tile,),
        in_specs=[pl.BlockSpec((back.shape[0], tile, FINE), lambda i: (0, i, 0))]
        + [block] * 3
        + [pl.BlockSpec((width, width), lambda i: (0, 0))],
        out_specs=[block] * 3,
        out_shape=[jax.ShapeDtypeStruct((rows, width), jnp.float32)] * 3,
        compiler_params=pltpu.CompilerParams(vmem_limit_bytes=VMEM_BYTES),
        cost_estimate=pl.CostEstimate(
            flops=8 * rows * width * width, bytes_accessed=32 * rows * width, transcendentals=0
        ),
        name="unpack",
    )(back, k_gate, values, grad_out, table)


def spectral(pair, filt, own, chans):
    length = pair.shape[0]
    first, last, fine = kernel_tables(length)
    spread, fold = fold_tables(own, chans)
    return pl.pallas_call(
        spectral_kernel,
        in_specs=[pl.BlockSpec(memory_space=pltpu.VMEM)] * 7,
        out_specs=[pl.BlockSpec(memory_space=pltpu.VMEM)] * 2,
        out_shape=[
            jax.ShapeDtypeStruct(pair.shape, jnp.float32),
            jax.ShapeDtypeStruct(filt.shape, jnp.float32),
        ],
        scratch_shapes=[
            pltpu.VMEM((length, FINE), jnp.float32),
            pltpu.VMEM((2 * length, FINE), jnp.float32),
            pltpu.VMEM((2 * length, FINE), jnp.float32),
        ],
        compiler_params=pltpu.CompilerParams(vmem_limit_bytes=VMEM_BYTES),
        cost_estimate=pl.CostEstimate(
            flops=16_000_000_000, bytes_accessed=24 << 20, transcendentals=0
        ),
        name="spectral",
    )(pair, filt, jnp.asarray(first), jnp.asarray(last), jnp.asarray(fine),
      jnp.asarray(spread), jnp.asarray(fold))


def local(q_gate, k_gate, values, filter_raw, grad_out):
    rows, width = q_gate.shape
    nfilt = filter_raw.shape[1]
    shards = lax.axis_size("seq")
    length = rows * shards
    repeats = width // nfilt
    own = nfilt // shards
    chans = repeats * own
    scale = float(length) ** (-0.5)
    n1 = length // FINE
    first, last, tw_cos, tw_sin, ahead, back = tables(length)
    tw_cos = tw_cos[None, :, :, None][0]
    tw_sin = tw_sin[None, :, :, None][0]

    def split(block):
        groups = block.shape[1] // nfilt
        parts = block.reshape(rows, groups, shards, own)
        return parts.transpose(2, 0, 1, 3).reshape(shards, rows, groups * own)

    def merge(parts):
        groups = parts.shape[2] // own
        block = parts.reshape(shards, rows, groups, own).transpose(1, 2, 0, 3)
        return block.reshape(rows, groups * nfilt)

    def exchange(parts):
        return lax.all_to_all(parts, "seq", split_axis=0, concat_axis=0, tiled=True)

    if 2 * chans == FINE and n1 == 64:
        table = order_table(width, nfilt, own)
        filt = exchange(split(filter_raw * scale).reshape(shards, -1, FINE))
        pair = exchange(pack(k_gate, values, grad_out, q_gate, shards, jnp.asarray(table)))
        out, lags = spectral(
            pair.reshape(length, FINE), filt.reshape(-1, FINE), own, chans
        )
        out = exchange(out.reshape(shards, rows, FINE))
        lags = exchange(lags.reshape(shards, -1, FINE)).reshape(shards, rows, own)
        lags = lax.psum(merge(lags), "chan") * scale
        return tuple(unpack(out, k_gate, values, grad_out, jnp.asarray(table.T))) + (lags,)

    def forward(block):
        wide = block.shape[1]
        part = mul("pkn,nbw->pkbw", first, block.reshape(n1, FINE, wide))
        real, imag = part[0], part[1]
        turned = jnp.stack([real * tw_cos + imag * tw_sin, imag * tw_cos - real * tw_sin])
        return mul("opkn,ptnw->otkw", ahead, turned)

    def inverse(spec):
        wide = spec.shape[3]
        part = mul("opkn,ptnw->otkw", back, spec)
        real, imag = part[0], part[1]
        turned = jnp.stack([real * tw_cos - imag * tw_sin, imag * tw_cos + real * tw_sin])
        return mul("pkn,pkbw->nbw", last, turned).reshape(length, wide)

    pair = jnp.concatenate([split(k_gate * values), split(grad_out * q_gate)], axis=2)
    pair = exchange(pair).reshape(length, 2 * chans)
    filt = split(filter_raw * scale).reshape(shards, -1, FINE)
    filt = exchange(filt).reshape(length, own)

    spec = forward(pair)
    gr, gi = spec[0, :, :, :chans], spec[1, :, :, :chans]
    qr, qi = spec[0, :, :, chans:], spec[1, :, :, chans:]
    fspec = jnp.tile(forward(filt), (1, 1, 1, repeats))
    fr, fi = fspec[0], fspec[1]
    conv = jnp.stack([fr * gr - fi * gi, fr * gi + fi * gr])
    adj = jnp.stack([fr * qr + fi * qi, fr * qi - fi * qr])
    corr = jnp.stack([gr * qr + gi * qi, gr * qi - gi * qr])
    corr = corr.reshape(2, n1, FINE, repeats, own).sum(axis=3)
    out = inverse(jnp.concatenate([conv, adj], axis=3)).reshape(shards, rows, 2 * chans)
    lags = inverse(corr).reshape(shards, -1, FINE)
    out = exchange(out)
    lags = exchange(lax.psum(lags, "chan") * scale).reshape(shards, rows, own)

    grad_gated = merge(out[:, :, chans:])
    return (
        grad_out * merge(out[:, :, :chans]),
        grad_gated * values,
        grad_gated * k_gate,
        merge(lags),
    )


def solution(mesh):
    placed = P("seq", "chan")
    return jax.shard_map(
        local,
        mesh=mesh,
        in_specs=(placed, placed, placed, P("seq", None), placed),
        out_specs=(placed, placed, placed, P("seq", None)),
        check_vma=False,
    )
```

profile of v0, /device:TPU:11, one launch (start us, length us, event | category | flops | bytes accessed | tf_op | source)
XLA Modules:
  0.0 336.4 jit_solution(3244235892167672835)
XLA Ops:
  7.2 1.1 copy.24
  8.3 0.8 copy.25
  9.1 1.3 copy.26
  10.4 6.6 %all-to-all-start.1 = ((f32[16,32,128]{2,1,0:T(8,128)}), f32[16,32,128]{2,1,0:T(8,128)S(1)}, u32[]{:S(2)}, u32[]{:S(2)}) async-start(f32[16,32,128]{2,1,0:T(8,128)} %copy.26), calls=%async_computation.1 | async-start | bytes 524288 | tf_op jit(solution)/shard_map/all_to_all | solution.py:282
  17.0 9.7 %pack.1 = f32[16,512,128]{2,1,0:T(8,128)} custom-call(f32[512,1024]{1,0:T(8,128)} %k_ref.3, f32[512,1024]{1,0:T(8,128)} %v_ref.3, f32[512,1024]{1,0:T(8,128)} %o_ref.3, f32[512,1024]{1,0:T(8,128)} %q_ref.1, bf16[1024,1024]{1,0:T(8,128)(2,1)} %constant.16.clone.table_ref), custom_call_target="tpu_custom_call" | custom-call | flops 4294967296 | bytes 12582912 | tf_op jit(solution)/shard_map/pack/pallas_call | solution.py:197
  26.7 0.0 all-to-all-done.1
  26.7 0.0 copy-start
  26.7 98.4 %all_to_all.20 = f32[16,512,128]{2,1,0:T(8,128)} all-to-all(f32[16,512,128]{2,1,0:T(8,128)} %pack.1), channel_id=1, replica_groups=mesh['seq'=16,'chan'=2] {'seq'}, dimensions={0} | all-to-all | bytes 8388608 | tf_op jit(solution)/shard_map/all_to_all | solution.py:282
  125.1 0.0 copy-done
  125.1 82.5 %spectral.1 = (f32[8192,128]{1,0:T(8,128)}, f32[512,128]{1,0:T(8,128)}) custom-call(f32[8192,128]{1,0:T(8,128)} %bitcast.16, f32[512,128]{1,0:T(8,128)} %bitcast.18, bf16[128,128,192]{2,1,0:T(8,128)(2,1)} %constant.17.clone.first_ref, bf16[128,64,384]{2,1,0:T(8,128)(2,1)} %constant.18.clone.last_ref, bf16[4,256,256]{2,1,0:T(8,128)(2,1)} %constant.19.clone.fine_ref, ...), custom_call_target="tpu_custom_call" | custom-call | flops 16000000000 | bytes 25165824 | tf_op jit(solution)/shard_map/spectral/pallas_call | solution.py:235
  207.6 13.3 %all_to_all.21 = f32[16,32,128]{2,1,0:T(8,128)S(1)} all-to-all(f32[16,32,128]{2,1,0:T(8,128)} %bitcast.19), channel_id=1, replica_groups=mesh['seq'=16,'chan'=2] {'seq'}, dimensions={0} | all-to-all | bytes 524288 | tf_op jit(solution)/shard_map/all_to_all | solution.py:282
  220.9 6.5 %all-to-all-start.2 = ((f32[16,512,128]{2,1,0:T(8,128)}), f32[16,512,128]{2,1,0:T(8,128)}, u32[]{:S(2)}, u32[]{:S(2)}) async-start(f32[16,512,128]{2,1,0:T(8,128)} %bitcast.15), calls=%async_computation.2 | async-start | bytes 8388608 | tf_op jit(solution)/shard_map/all_to_all | solution.py:282
  227.4 0.0 all-reduce.2.cloned.1.call-start
  227.4 0.6 copy.27
  228.0 1.5 copy.28
  229.5 0.0 all-reduce.2.cloned.1.call-update
  229.5 25.0 %all-reduce.2.cloned.1.call-done = f32[512,128]{0,1:T(8,128)} async-done(((f32[512,128]{0,1:T(8,128)}), f32[512,128]{0,1:T(8,128)}) %all-reduce.2.cloned.1.call-update) | async-done | bytes 262160 | tf_op jit(solution)/shard_map/psum | solution.py:293
  254.5 1.0 broadcast_multiply_fusion
  255.5 0.8 copy.29
  256.3 63.6 %all-to-all-done.2.in_ref = f32[16,512,128]{2,1,0:T(8,128)} async-done(((f32[16,512,128]{2,1,0:T(8,128)}), f32[16,512,128]{2,1,0:T(8,128)}, u32[]{:S(2)}, u32[]{:S(2)}) %all-to-all-start.2) | async-done | bytes 4194336 | tf_op jit(solution)/shard_map/all_to_all | solution.py:282
  319.9 9.7 %unpack.1 = (f32[512,1024]{1,0:T(8,128)}, f32[512,1024]{1,0:T(8,128)}, f32[512,1024]{1,0:T(8,128)}) custom-call(f32[16,512,128]{2,1,0:T(8,128)} %all-to-all-done.2.in_ref, f32[512,1024]{1,0:T(8,128)} %k_ref.3, f32[512,1024]{1,0:T(8,128)} %v_ref.3, f32[512,1024]{1,0:T(8,128)} %o_ref.3, bf16[1024,1024]{1,0:T(8,128)(2,1)} %constant.22.clone.table_ref), custom_call_target="tpu_custom_call" | custom-call | flops 4294967296 | bytes 16777216 | tf_op jit(solution)/shard_map/unpack/pallas_call | solution.py:215
  (1 shorter events, 0.0 us)
Async XLA Ops:
  10.4 16.3 %all-to-all-start.1 = ((f32[16,32,128]{2,1,0:T(8,128)}), f32[16,32,128]{2,1,0:T(8,128)S(1)}, u32[]{:S(2)}, u32[]{:S(2)}) async-start(f32[16,32,128]{2,1,0:T(8,128)} %copy.26), calls=%async_computation.1 | async-start | bytes 524288 | tf_op jit(solution)/shard_map/all_to_all | solution.py:282
  26.7 98.4 %copy-start = (f32[16,32,128]{2,1,0:T(8,128)}, f32[16,32,128]{2,1,0:T(8,128)S(1)}, u32[]{:S(2)}) copy-start(f32[16,32,128]{2,1,0:T(8,128)S(1)} %all-to-all-done.1) | copy-start | bytes 786436
  220.9 99.0 %all-to-all-start.2 = ((f32[16,512,128]{2,1,0:T(8,128)}), f32[16,512,128]{2,1,0:T(8,128)}, u32[]{:S(2)}, u32[]{:S(2)}) async-start(f32[16,512,128]{2,1,0:T(8,128)} %bitcast.15), calls=%async_computation.2 | async-start | bytes 8388608 | tf_op jit(solution)/shard_map/all_to_all | solution.py:282
  227.4 27.1 %all-reduce.2.cloned.1.call-start = ((), (), s32[]{:S(2)}) async-start(), calls=%async_computation.4 | async-start | bytes 524288 | tf_op jit(solution)/shard_map/psum | solution.py:293
Sparse Core Ops, SparseCore 0:
  231.1 23.3 all-reduce.1
where the time goes:
time: 337 us; the launch traced here: 336 us
  blocking collectives  112 us (33%)
  Pallas kernels  102 us (30%)
  waiting for transfers between devices  88.5 us (26%)
  between operations  14.1 us (4%)
  starting transfers between devices  13.1 us (4%)
  local copies, waits for them, and re-layouts  6.14 us (2%)
    all_to_all x2, blocking collectives, exchange(): return lax.all_to_all(parts, 'seq', split_axis=0, concat_axis=0, tiled=True)  112 us
    pallas_call x1, Pallas kernels, spectral(): pl.pallas_call(spectral_kernel, in_specs=[pl.BlockSpec(memory_space=pltpu...  82.5 us
    all_to_all x2, waiting for transfers between devices, exchange(): return lax.all_to_all(parts, 'seq', split_axis=0, concat_axis=0, tiled=True)  63.6 us
    psum x1, waiting for transfers between devices, local(): lags = lax.psum(merge(lags), 'chan') * scale  25 us
    all_to_all x2, starting transfers between devices, exchange(): return lax.all_to_all(parts, 'seq', split_axis=0, concat_axis=0, tiled=True)  13.1 us
    pallas_call x1, Pallas kernels, pack(): pl.pallas_call(pack_kernel, grid=(rows // tile,), in_specs=[block] * 4 +...  9.73 us
    pallas_call x1, Pallas kernels, unpack(): pl.pallas_call(unpack_kernel, grid=(rows // tile,), in_specs=[pl.BlockSpe...  9.66 us
  transfers between devices with their start and end apart: 3, of which 2 were waited for; matrix products, arithmetic and copies ran while one was open for 1% of the time, Pallas kernels for 3%

commit v1 on v0

--- a/solution.py
+++ b/solution.py
@@ -113,78 +113,127 @@
     gv_ref[...] = moved[1] * k_ref[...]
 
 
-def spectral_kernel(
-    pair_ref, filt_ref, first_ref, last_ref, fine_ref, spread_ref, fold_ref,
-    out_ref, lags_ref, wide_ref, spec_a, spec_b,
-):
-    length = pair_ref.shape[0]
-    n1 = length // FINE
+STEPS = 8
+PITCH = FINE + 8
+
+
+def fine(fine_ref, which, re, im):
+    high, rest = split_value(jnp.concatenate([re, im], axis=0))
+    top, bottom = fine_ref[2 * which], fine_ref[2 * which + 1]
+    return dot(top, high) + (dot(bottom, high) + dot(top, rest))
+
+
+def coarse(step, table_ref, src_ref, lines_in, dst_ref, lines_out):
+    count = table_ref.shape[0]
+    for j in range(count):
+        n2 = step * count + j
+        high, rest = split_value(src_ref[pl.ds(n2, lines_in, stride=PITCH), :])
+        dst_ref[pl.ds(n2, lines_out, stride=PITCH), :] = dot(
+            table_ref[j], jnp.concatenate([high, high, rest], axis=0)
+        )
+
+
+def lines(spec_ref, n1, k1):
+    at = [pl.multiple_of(p * PITCH, 8) for p in (k1, k1 + n1)]
+    return [pl.ds(p, FINE) for p in at]
+
+
+def filter_kernel(filt_ref, first_ref, fine_ref, spread_ref, out_ref, wide_ref, space_ref, spec_ref):
+    i = pl.program_id(0)
+    n1 = space_ref.shape[0] // PITCH
     spots = spread_ref.shape[0]
-    short = length // spots
-
-    fh, fl = split_value(filt_ref[...])
-    for j in range(spots):
-        e = spread_ref[j]
-        wide_ref[pl.ds(j, short, stride=spots), :] = dot(fh, e) + dot(fl, e)
-
-    def ahead(n2, carry):
-        x = jnp.concatenate(
-            [r[pl.ds(n2, n1, stride=FINE), :] for r in (pair_ref, wide_ref)], axis=1
-        )
-        high, rest = split_value(x)
-        y = dot(first_ref[n2], jnp.concatenate([high, high, rest], axis=0))
-        spec_a[pl.ds(n2, 2 * n1, stride=FINE), :] = y[:, :FINE]
-        spec_b[pl.ds(n2, 2 * n1, stride=FINE), :] = y[:, FINE:]
-        return carry
-
-    lax.fori_loop(0, FINE, ahead, 0, unroll=4)
-
-    sign = jnp.where(low_lanes(FINE), 1.0, -1.0)
-
-    def fine(which, re, im):
-        high, rest = split_value(jnp.concatenate([re, im], axis=0))
-        top, bottom = fine_ref[2 * which], fine_ref[2 * which + 1]
-        return dot(top, high) + (dot(bottom, high) + dot(top, rest))
-
-    def middle(k1, carry):
-        at_re = pl.ds(pl.multiple_of(k1 * FINE, FINE), FINE)
-        at_im = pl.ds(pl.multiple_of((k1 + n1) * FINE, FINE), FINE)
-        z = fine(
-            0,
-            jnp.concatenate([spec_a[at_re, :], spec_b[at_re, :]], axis=1),
-            jnp.concatenate([spec_a[at_im, :], spec_b[at_im, :]], axis=1),
-        )
-        pr, fr = z[:FINE, :FINE], z[:FINE, FINE:]
-        pi, fi = z[FINE:, :FINE], z[FINE:, FINE:] * sign
-        qr, qi = pltpu.roll(pr, FINE // 2, 1), pltpu.roll(pi, FINE // 2, 1)
-        re = jnp.concatenate([fr * pr - fi * pi, pr * qr + pi * qi], axis=1)
-        im = jnp.concatenate([fr * pi + fi * pr, pr * qi - pi * qr], axis=1)
-        w = fine(1, re, im)
-        spec_a[at_re, :] = w[:FINE, :FINE]
-        spec_b[at_re, :] = w[:FINE, FINE:]
-        spec_a[at_im, :] = w[FINE:, :FINE]
-        spec_b[at_im, :] = w[FINE:, FINE:]
-        return carry
-
-    lax.fori_loop(0, n1, middle, 0, unroll=2)
-
-    def behind(n2, carry):
-        x = jnp.concatenate(
-            [r[pl.ds(n2, 2 * n1, stride=FINE), :] for r in (spec_a, spec_b)], axis=1
-        )
-        high, rest = split_value(x)
-        y = dot(last_ref[n2], jnp.concatenate([high, high, rest], axis=0))
-        out_ref[pl.ds(n2, n1, stride=FINE), :] = y[:, :FINE]
-        wide_ref[pl.ds(n2, n1, stride=FINE), :] = y[:, FINE:]
-        return carry
-
-    lax.fori_loop(0, FINE, behind, 0, unroll=4)
-
-    total = jnp.zeros((short, FINE), jnp.float32)
-    for j in range(spots):
-        high, rest = split_value(wide_ref[pl.ds(j, short, stride=spots), :])
-        total += dot(high, fold_ref[j]) + dot(rest, fold_ref[j])
-    lags_ref[...] = total
+    group = out_ref.shape[1]
+
+    @pl.when(i == 0)
+    def _():
+        high, rest = split_value(filt_ref[...])
+        short = filt_ref.shape[0]
+        for j in range(spots):
+            e = spread_ref[j]
+            wide_ref[pl.ds(j, short, stride=spots), :] = dot(high, e) + dot(rest, e)
+        for line in range(n1):
+            space_ref[line * PITCH : line * PITCH + FINE, :] = wide_ref[line * FINE : (line + 1) * FINE, :]
+
+    @pl.when(i < STEPS)
+    def _():
+        coarse(i, first_ref, space_ref, n1, spec_ref, 2 * n1)
+
+    @pl.when(i >= STEPS)
+    def _():
+        for j in range(group):
+            at_re, at_im = lines(spec_ref, n1, (i - STEPS) * group + j)
+            z = fine(fine_ref, 0, spec_ref[at_re, :], spec_ref[at_im, :])
+            out_ref[0, j] = z[:FINE]
+            out_ref[1, j] = z[FINE:]
+
+
+def main_kernel(pair_ref, fspec_ref, first_ref, last_ref, fine_ref, out_ref, corr_ref, space_ref, spec_ref):
+    i = pl.program_id(0)
+    n1 = space_ref.shape[0] // PITCH
+    group = fspec_ref.shape[1]
+
+    @pl.when(i == 0)
+    def _():
+        for line in range(n1):
+            space_ref[line * PITCH : line * PITCH + FINE, :] = pair_ref[line * FINE : (line + 1) * FINE, :]
+
+    @pl.when(i < STEPS)
+    def _():
+        coarse(i, first_ref, space_ref, n1, spec_ref, 2 * n1)
+
+    @pl.when((i >= STEPS) & (i < 2 * STEPS))
+    def _():
+        sign = jnp.where(low_lanes(FINE), 1.0, -1.0)
+        for j in range(group):
+            at_re, at_im = lines(spec_ref, n1, (i - STEPS) * group + j)
+            z = fine(fine_ref, 0, spec_ref[at_re, :], spec_ref[at_im, :])
+            pr, pi = z[:FINE], z[FINE:]
+            fr, fi = fspec_ref[0, j], fspec_ref[1, j] * sign
+            qr, qi = pltpu.roll(pr, FINE // 2, 1), pltpu.roll(pi, FINE // 2, 1)
+            corr_ref[0, j] = pr * qr + pi * qi
+            corr_ref[1, j] = pr * qi - pi * qr
+            w = fine(fine_ref, 1, fr * pr - fi * pi, fr * pi + fi * pr)
+            spec_ref[at_re, :] = w[:FINE]
+            spec_ref[at_im, :] = w[FINE:]
+
+    @pl.when(i >= 2 * STEPS)
+    def _():
+        coarse(i - 2 * STEPS, last_ref, spec_ref, 2 * n1, space_ref, n1)
+
+    @pl.when(i == 3 * STEPS - 1)
+    def _():
+        for line in range(n1):
+            out_ref[line * FINE : (line + 1) * FINE, :] = space_ref[line * PITCH : line * PITCH + FINE, :]
+
+
+def lags_kernel(corr_ref, last_ref, fine_ref, fold_ref, lags_ref, wide_ref, space_ref, spec_ref):
+    i = pl.program_id(0)
+    n1 = space_ref.shape[0] // PITCH
+    spots = fold_ref.shape[0]
+    group = corr_ref.shape[1]
+
+    @pl.when(i < STEPS)
+    def _():
+        for j in range(group):
+            at_re, at_im = lines(spec_ref, n1, i * group + j)
+            w = fine(fine_ref, 1, corr_ref[0, j], corr_ref[1, j])
+            spec_ref[at_re, :] = w[:FINE]
+            spec_ref[at_im, :] = w[FINE:]
+
+    @pl.when(i >= STEPS)
+    def _():
+        coarse(i - STEPS, last_ref, spec_ref, 2 * n1, space_ref, n1)
+
+    @pl.when(i == 2 * STEPS - 1)
+    def _():
+        for line in range(n1):
+            wide_ref[line * FINE : (line + 1) * FINE, :] = space_ref[line * PITCH : line * PITCH + FINE, :]
+        short = lags_ref.shape[0]
+        total = jnp.zeros((short, FINE), jnp.float32)
+        for j in range(spots):
+            high, rest = split_value(wide_ref[pl.ds(j, short, stride=spots), :])
+            total += dot(high, fold_ref[j]) + dot(rest, fold_ref[j])
+        lags_ref[...] = total
 
 
 VMEM_BYTES = 60 << 20
@@ -228,30 +277,67 @@
     )(back, k_gate, values, grad_out, table)
 
 
-def spectral(pair, filt, own, chans):
-    length = pair.shape[0]
-    first, last, fine = kernel_tables(length)
-    spread, fold = fold_tables(own, chans)
+def whole(array):
+    return pl.BlockSpec(array.shape, lambda i: (0,) * len(array.shape))
+
+
+def phase(array, axis, start):
+    block = tuple(d // STEPS if a == axis else d for a, d in enumerate(array.shape))
+
+    def index(i):
+        at = jnp.clip(i - start, 0, STEPS - 1)
+        return tuple(at if a == axis else 0 for a in range(len(block)))
+
+    return pl.BlockSpec(block, index)
+
+
+def stepped(kernel, phases, ins, in_specs, outs, out_specs, scratch, flops, name):
     return pl.pallas_call(
-        spectral_kernel,
-        in_specs=[pl.BlockSpec(memory_space=pltpu.VMEM)] * 7,
-        out_specs=[pl.BlockSpec(memory_space=pltpu.VMEM)] * 2,
-        out_shape=[
-            jax.ShapeDtypeStruct(pair.shape, jnp.float32),
-            jax.ShapeDtypeStruct(filt.shape, jnp.float32),
-        ],
-        scratch_shapes=[
-            pltpu.VMEM((length, FINE), jnp.float32),
-            pltpu.VMEM((2 * length, FINE), jnp.float32),
-            pltpu.VMEM((2 * length, FINE), jnp.float32),
-        ],
+        kernel,
+        grid=(phases * STEPS,),
+        in_specs=in_specs,
+        out_specs=out_specs,
+        out_shape=outs,
+        scratch_shapes=[pltpu.VMEM((rows, FINE), jnp.float32) for rows in scratch],
         compiler_params=pltpu.CompilerParams(vmem_limit_bytes=VMEM_BYTES),
         cost_estimate=pl.CostEstimate(
-            flops=16_000_000_000, bytes_accessed=24 << 20, transcendentals=0
+            flops=flops, bytes_accessed=24 << 20, transcendentals=0
         ),
-        name="spectral",
-    )(pair, filt, jnp.asarray(first), jnp.asarray(last), jnp.asarray(fine),
-      jnp.asarray(spread), jnp.asarray(fold))
+        name=name,
+    )(*ins)
+
+
+def spectral(length, own, chans):
+    n1 = length // FINE
+    first, last, mats = (jnp.asarray(t) for t in kernel_tables(length))
+    spread, fold = (jnp.asarray(t) for t in fold_tables(own, chans))
+    spec = jax.ShapeDtypeStruct((2, n1, FINE, FINE), jnp.float32)
+    space = jax.ShapeDtypeStruct((length, FINE), jnp.float32)
+    packed = jax.ShapeDtypeStruct((length * own // FINE, FINE), jnp.float32)
+    padded = [n1 * PITCH, 2 * n1 * PITCH]
+
+    def filter_stage(filt):
+        return stepped(
+            filter_kernel, 2, (filt, first, mats, spread),
+            [whole(filt), phase(first, 0, 0), whole(mats), whole(spread)],
+            spec, phase(spec, 1, STEPS), [length] + padded, 15_000_000_000, "filter_spectrum",
+        )
+
+    def main_stage(pair, fspec):
+        return stepped(
+            main_kernel, 3, (pair, fspec, first, last, mats),
+            [whole(pair), phase(fspec, 1, STEPS), phase(first, 0, 0), phase(last, 0, 2 * STEPS), whole(mats)],
+            [space, spec], [whole(space), phase(spec, 1, STEPS)], padded, 30_000_000_000, "pair_stage",
+        )
+
+    def lags_stage(corr):
+        return stepped(
+            lags_kernel, 2, (corr, last, mats, fold),
+            [phase(corr, 1, 0), phase(last, 0, STEPS), whole(mats), whole(fold)],
+            packed, whole(packed), [length] + padded, 15_000_000_000, "lags",
+        )
+
+    return filter_stage, main_stage, lags_stage
 
 
 def local(q_gate, k_gate, values, filter_raw, grad_out):
@@ -285,12 +371,12 @@
         table = order_table(width, nfilt, own)
         filt = exchange(split(filter_raw * scale).reshape(shards, -1, FINE))
         pair = exchange(pack(k_gate, values, grad_out, q_gate, shards, jnp.asarray(table)))
-        out, lags = spectral(
-            pair.reshape(length, FINE), filt.reshape(-1, FINE), own, chans
-        )
+        filter_stage, main_stage, lags_stage = spectral(length, own, chans)
+        fspec = filter_stage(filt.reshape(-1, FINE))
+        out, corr = main_stage(pair.reshape(length, FINE), fspec)
         out = exchange(out.reshape(shards, rows, FINE))
-        lags = exchange(lags.reshape(shards, -1, FINE)).reshape(shards, rows, own)
-        lags = lax.psum(merge(lags), "chan") * scale
+        lags = lax.psum(lags_stage(corr), "chan") * scale
+        lags = merge(exchange(lags.reshape(shards, -1, FINE)).reshape(shards, rows, own))
         return tuple(unpack(out, k_gate, values, grad_out, jnp.asarray(table.T))) + (lags,)
 
     def forward(block):

time: 337 us -> 344 us (1.021)
  waiting for transfers between devices: 88.5 us -> 186 us
  blocking collectives: 112 us -> 14.6 us
  starting transfers between devices: 13.1 us -> 19.3 us
    all_to_all x2 -> x3, waiting for transfers between devices: 63.6 us -> 163 us  [exchange(): return lax.all_to_all(parts, 'seq', split_axis=0, concat_axis=0, tiled=True)]
    all_to_all x2 -> x1, blocking collectives: 112 us -> 14.6 us  [exchange(): return lax.all_to_all(parts, 'seq', split_axis=0, concat_axis=0, tiled=True)]
    all_to_all x2 -> x3, starting transfers between devices: 13.1 us -> 19.1 us  [exchange(): return lax.all_to_all(parts, 'seq', split_axis=0, concat_axis=0, tiled=True)]
    pallas_call x1 -> x3, Pallas kernels: 82.5 us -> 83 us  [stepped(): pl.pallas_call(kernel, grid=(phases * STEPS,), in_specs=in_specs, out_spe...]
  transfers between devices with their start and end apart: 3 -> 4, of which waited for: 2 -> 3; matrix products, arithmetic and copies ran while one was open for 1% -> 1% of each run, Pallas kernels for 3% -> 8%
where the time goes in v1:
time: 344 us; the launch traced here: 343 us
  waiting for transfers between devices  186 us (54%)
  Pallas kernels  102 us (30%)
  starting transfers between devices  19.3 us (6%)
  blocking collectives  14.6 us (4%)
  between operations  14.1 us (4%)
  local copies, waits for them, and re-layouts  5.18 us (2%)
    all_to_all x3, waiting for transfers between devices, exchange(): return lax.all_to_all(parts, 'seq', split_axis=0, concat_axis=0, tiled=True)  163 us
    pallas_call x3, Pallas kernels, stepped(): pl.pallas_call(kernel, grid=(phases * STEPS,), in_specs=in_specs, out_spe...  83 us
    psum x1, waiting for transfers between devices, local(): lags = lax.psum(lags_stage(corr), 'chan') * scale  22.4 us
    all_to_all x3, starting transfers between devices, exchange(): return lax.all_to_all(parts, 'seq', split_axis=0, concat_axis=0, tiled=True)  19.1 us
    all_to_all x1, blocking collectives, exchange(): return lax.all_to_all(parts, 'seq', split_axis=0, concat_axis=0, tiled=True)  14.6 us
    pallas_call x1, Pallas kernels, pack(): pl.pallas_call(pack_kernel, grid=(rows // tile,), in_specs=[block] * 4 +...  9.77 us
    pallas_call x1, Pallas kernels, unpack(): pl.pallas_call(unpack_kernel, grid=(rows // tile,), in_specs=[pl.BlockSpe...  9.66 us
  transfers between devices with their start and end apart: 4, of which 3 were waited for; matrix products, arithmetic and copies ran while one was open for 1% of the time, Pallas kernels for 8%

profile of v1, /device:TPU:11, one launch (start us, length us, event | category | flops | bytes accessed | tf_op | source)
XLA Modules:
  0.0 343.2 jit_solution(13369072935852749524)
XLA Ops:
  7.2 1.0 broadcast_multiply_fusion.1
  8.1 0.1 copy.23
  8.3 0.8 copy.24
  9.1 1.3 copy.25
  10.4 6.6 %all-to-all-start.1 = ((f32[16,32,128]{2,1,0:T(8,128)}), f32[16,32,128]{2,1,0:T(8,128)S(1)}, u32[]{:S(2)}, u32[]{:S(2)}) async-start(f32[16,32,128]{2,1,0:T(8,128)} %copy.25), calls=%async_computation.1 | async-start | bytes 524288 | tf_op jit(solution)/shard_map/all_to_all | solution.py:368
  17.0 9.8 %pack.1 = f32[16,512,128]{2,1,0:T(8,128)} custom-call(f32[512,1024]{1,0:T(8,128)} %k_ref.3, f32[512,1024]{1,0:T(8,128)} %v_ref.3, f32[512,1024]{1,0:T(8,128)} %o_ref.3, f32[512,1024]{1,0:T(8,128)} %q_ref.1, bf16[1024,1024]{1,0:T(8,128)(2,1)} %constant.16.clone.table_ref), custom_call_target="tpu_custom_call" | custom-call | flops 4294967296 | bytes 12582912 | tf_op jit(solution)/shard_map/pack/pallas_call | solution.py:246
  26.8 0.0 all-to-all-done.1
  26.8 0.7 copy-done
  27.5 6.0 %all-to-all-start = ((f32[16,512,128]{2,1,0:T(8,128)}), f32[16,512,128]{2,1,0:T(8,128)}, u32[]{:S(2)}, u32[]{:S(2)}) async-start(f32[16,512,128]{2,1,0:T(8,128)} %pack.1), calls=%async_computation | async-start | bytes 8388608 | tf_op jit(solution)/shard_map/all_to_all | solution.py:368
  33.5 0.2 all-reduce.2.cloned.1.call-start
  33.7 19.2 %filter_spectrum.1.fspec_ref = f32[2,64,128,128]{3,2,1,0:T(8,128)} custom-call(f32[512,128]{1,0:T(8,128)} %bitcast.18, bf16[128,128,192]{2,1,0:T(8,128)(2,1)} %constant.17.clone.first_ref, bf16[4,256,256]{2,1,0:T(8,128)(2,1)} %constant.19.clone.fine_ref, bf16[16,128,128]{2,1,0:T(8,128)(2,1)} %constant.20.clone.spread_ref), custom_call_target="tpu_custom_call" | custom-call | flops 15000000512 | bytes 25165824 | tf_op jit(solution)/shard_map/filter_spectrum/pallas_call | solution.py:295
  52.9 73.0 %all-to-all-done = f32[16,512,128]{2,1,0:T(8,128)} async-done(((f32[16,512,128]{2,1,0:T(8,128)}), f32[16,512,128]{2,1,0:T(8,128)}, u32[]{:S(2)}, u32[]{:S(2)}) %all-to-all-start) | async-done | bytes 4194336 | tf_op jit(solution)/shard_map/all_to_all | solution.py:368
  125.9 44.1 %pair_stage.1 = (f32[8192,128]{1,0:T(8,128)}, f32[2,64,128,128]{3,2,1,0:T(8,128)}) custom-call(f32[8192,128]{1,0:T(8,128)} %bitcast.pair_ref, f32[2,64,128,128]{3,2,1,0:T(8,128)} %filter_spectrum.1.fspec_ref, bf16[128,128,192]{2,1,0:T(8,128)(2,1)} %constant.17.clone.first_ref, bf16[128,64,384]{2,1,0:T(8,128)(2,1)} %constant.18.clone.last_ref, ...), custom_call_target="tpu_custom_call" | custom-call | flops 30000001024 | bytes 25165824 | tf_op jit(solution)/shard_map/pair_stage/pallas_call | solution.py:295
  170.0 19.8 %lags.1 = f32[512,128]{1,0:T(8,128)} custom-call(f32[2,64,128,128]{3,2,1,0:T(8,128)} %get-tuple-element.13.corr_ref, bf16[128,64,384]{2,1,0:T(8,128)(2,1)} %constant.18.clone.last_ref, bf16[4,256,256]{2,1,0:T(8,128)(2,1)} %constant.19.clone.fine_ref, bf16[16,128,128]{2,1,0:T(8,128)(2,1)} %constant.21.clone.fold_ref), custom_call_target="tpu_custom_call" | custom-call | flops 15000000512 | bytes 25165824 | tf_op jit(solution)/shard_map/lags/pallas_call | solution.py:295
  189.8 0.0 all-reduce.2.cloned.1.call-update
  189.8 22.4 %all-reduce.2.cloned.1.call-done = f32[512,128]{1,0:T(8,128)} async-done(((f32[512,128]{1,0:T(8,128)}), f32[512,128]{1,0:T(8,128)}) %all-reduce.2.cloned.1.call-update) | async-done | bytes 262160 | tf_op jit(solution)/shard_map/psum | solution.py:378
  212.2 1.0 broadcast_multiply_fusion
  213.2 14.6 %all_to_all.20 = f32[16,32,128]{2,1,0:T(8,128)S(1)} all-to-all(f32[16,32,128]{2,1,0:T(8,128)S(1)} %bitcast.17), channel_id=1, replica_groups=mesh['seq'=16,'chan'=2] {'seq'}, dimensions={0} | all-to-all | bytes 524288 | tf_op jit(solution)/shard_map/all_to_all | solution.py:368
  227.7 6.5 %all-to-all-start.2 = ((f32[16,512,128]{2,1,0:T(8,128)}), f32[16,512,128]{2,1,0:T(8,128)}, u32[]{:S(2)}, u32[]{:S(2)}) async-start(f32[16,512,128]{2,1,0:T(8,128)} %bitcast.14), calls=%async_computation.2 | async-start | bytes 8388608 | tf_op jit(solution)/shard_map/all_to_all | solution.py:368
  234.2 0.6 copy.26
  234.8 0.8 copy.27
  235.6 0.8 copy.28
  236.5 90.3 %all-to-all-done.2.in_ref = f32[16,512,128]{2,1,0:T(8,128)} async-done(((f32[16,512,128]{2,1,0:T(8,128)}), f32[16,512,128]{2,1,0:T(8,128)}, u32[]{:S(2)}, u32[]{:S(2)}) %all-to-all-start.2) | async-done | bytes 4194336 | tf_op jit(solution)/shard_map/all_to_all | solution.py:368
  326.7 9.7 %unpack.1 = (f32[512,1024]{1,0:T(8,128)}, f32[512,1024]{1,0:T(8,128)}, f32[512,1024]{1,0:T(8,128)}) custom-call(f32[16,512,128]{2,1,0:T(8,128)} %all-to-all-done.2.in_ref, f32[512,1024]{1,0:T(8,128)} %k_ref.3, f32[512,1024]{1,0:T(8,128)} %v_ref.3, f32[512,1024]{1,0:T(8,128)} %o_ref.3, bf16[1024,1024]{1,0:T(8,128)(2,1)} %constant.22.clone.table_ref), custom_call_target="tpu_custom_call" | custom-call | flops 4294967296 | bytes 16777216 | tf_op jit(solution)/shard_map/unpack/pallas_call | solution.py:264
  (1 shorter events, 0.0 us)
Async XLA Ops:
  10.4 16.3 %all-to-all-start.1 = ((f32[16,32,128]{2,1,0:T(8,128)}), f32[16,32,128]{2,1,0:T(8,128)S(1)}, u32[]{:S(2)}, u32[]{:S(2)}) async-start(f32[16,32,128]{2,1,0:T(8,128)} %copy.25), calls=%async_computation.1 | async-start | bytes 524288 | tf_op jit(solution)/shard_map/all_to_all | solution.py:368
  26.8 0.7 copy-start
  27.5 98.5 %all-to-all-start = ((f32[16,512,128]{2,1,0:T(8,128)}), f32[16,512,128]{2,1,0:T(8,128)}, u32[]{:S(2)}, u32[]{:S(2)}) async-start(f32[16,512,128]{2,1,0:T(8,128)} %pack.1), calls=%async_computation | async-start | bytes 8388608 | tf_op jit(solution)/shard_map/all_to_all | solution.py:368
  33.5 178.7 %all-reduce.2.cloned.1.call-start = ((), (), s32[]{:S(2)}) async-start(), calls=%async_computation.4 | async-start | bytes 524288 | tf_op jit(solution)/shard_map/psum | solution.py:378
  227.7 99.0 %all-to-all-start.2 = ((f32[16,512,128]{2,1,0:T(8,128)}), f32[16,512,128]{2,1,0:T(8,128)}, u32[]{:S(2)}, u32[]{:S(2)}) async-start(f32[16,512,128]{2,1,0:T(8,128)} %bitcast.14), calls=%async_computation.2 | async-start | bytes 8388608 | tf_op jit(solution)/shard_map/all_to_all | solution.py:368
Sparse Core Ops, SparseCore 0:
  189.9 22.2 all-reduce.1

commit v2 on v1

--- a/solution.py
+++ b/solution.py
@@ -56,7 +56,7 @@
     cos, sin = np.cos(fine), np.sin(fine)
     fwd = np.block([[cos, sin], [-sin, cos]]).astype(np.float32)
     inv = np.block([[cos, -sin], [sin, cos]]).astype(np.float32)
-    return first, last, np.stack(halves(fwd) + halves(inv))
+    return first, last, np.stack([np.concatenate(halves(m)) for m in (fwd, inv)])
 
 
 def fold_tables(own, chans):
@@ -119,8 +119,8 @@
 
 def fine(fine_ref, which, re, im):
     high, rest = split_value(jnp.concatenate([re, im], axis=0))
-    top, bottom = fine_ref[2 * which], fine_ref[2 * which + 1]
-    return dot(top, high) + (dot(bottom, high) + dot(top, rest))
+    both = dot(fine_ref[which], high)
+    return both[: 2 * FINE] + (both[2 * FINE :] + dot(fine_ref[which, : 2 * FINE, :], rest))
 
 
 def coarse(step, table_ref, src_ref, lines_in, dst_ref, lines_out):
@@ -133,6 +133,10 @@
         )
 
 
+def side_by_side(spec_ref, at):
+    return jnp.concatenate([spec_ref[a, :] for a in at], axis=1)
+
+
 def lines(spec_ref, n1, k1):
     at = [pl.multiple_of(p * PITCH, 8) for p in (k1, k1 + n1)]
     return [pl.ds(p, FINE) for p in at]
@@ -160,11 +164,12 @@
 
     @pl.when(i >= STEPS)
     def _():
-        for j in range(group):
-            at_re, at_im = lines(spec_ref, n1, (i - STEPS) * group + j)
-            z = fine(fine_ref, 0, spec_ref[at_re, :], spec_ref[at_im, :])
-            out_ref[0, j] = z[:FINE]
-            out_ref[1, j] = z[FINE:]
+        for j in range(0, group, 2):
+            at_re, at_im = zip(*(lines(spec_ref, n1, (i - STEPS) * group + j + e) for e in (0, 1)))
+            z = fine(fine_ref, 0, side_by_side(spec_ref, at_re), side_by_side(spec_ref, at_im))
+            for e in (0, 1):
+                out_ref[0, j + e] = z[:FINE, e * FINE : (e + 1) * FINE]
+                out_ref[1, j + e] = z[FINE:, e * FINE : (e + 1) * FINE]
 
 
 def main_kernel(pair_ref, fspec_ref, first_ref, last_ref, fine_ref, out_ref, corr_ref, space_ref, spec_ref):
@@ -184,17 +189,21 @@
     @pl.when((i >= STEPS) & (i < 2 * STEPS))
     def _():
         sign = jnp.where(low_lanes(FINE), 1.0, -1.0)
-        for j in range(group):
-            at_re, at_im = lines(spec_ref, n1, (i - STEPS) * group + j)
-            z = fine(fine_ref, 0, spec_ref[at_re, :], spec_ref[at_im, :])
-            pr, pi = z[:FINE], z[FINE:]
-            fr, fi = fspec_ref[0, j], fspec_ref[1, j] * sign
-            qr, qi = pltpu.roll(pr, FINE // 2, 1), pltpu.roll(pi, FINE // 2, 1)
-            corr_ref[0, j] = pr * qr + pi * qi
-            corr_ref[1, j] = pr * qi - pi * qr
-            w = fine(fine_ref, 1, fr * pr - fi * pi, fr * pi + fi * pr)
-            spec_ref[at_re, :] = w[:FINE]
-            spec_ref[at_im, :] = w[FINE:]
+        for j in range(0, group, 2):
+            at_re, at_im = zip(*(lines(spec_ref, n1, (i - STEPS) * group + j + e) for e in (0, 1)))
+            z = fine(fine_ref, 0, side_by_side(spec_ref, at_re), side_by_side(spec_ref, at_im))
+            prod = []
+            for e in (0, 1):
+                pr, pi = (z[p * FINE : (p + 1) * FINE, e * FINE : (e + 1) * FINE] for p in (0, 1))
+                fr, fi = fspec_ref[0, j + e], fspec_ref[1, j + e] * sign
+                qr, qi = pltpu.roll(pr, FINE // 2, 1), pltpu.roll(pi, FINE // 2, 1)
+                corr_ref[0, j + e] = pr * qr + pi * qi
+                corr_ref[1, j + e] = pr * qi - pi * qr
+                prod.append((fr * pr - fi * pi, fr * pi + fi * pr))
+            w = fine(fine_ref, 1, *(jnp.concatenate(part, axis=1) for part in zip(*prod)))
+            for e in (0, 1):
+                spec_ref[at_re[e], :] = w[:FINE, e * FINE : (e + 1) * FINE]
+                spec_ref[at_im[e], :] = w[FINE:, e * FINE : (e + 1) * FINE]
 
     @pl.when(i >= 2 * STEPS)
     def _():
@@ -214,11 +223,14 @@
 
     @pl.when(i < STEPS)
     def _():
-        for j in range(group):
-            at_re, at_im = lines(spec_ref, n1, i * group + j)
-            w = fine(fine_ref, 1, corr_ref[0, j], corr_ref[1, j])
-            spec_ref[at_re, :] = w[:FINE]
-            spec_ref[at_im, :] = w[FINE:]
+        for j in range(0, group, 2):
+            at_re, at_im = zip(*(lines(spec_ref, n1, i * group + j + e) for e in (0, 1)))
+            w = fine(
+                fine_ref, 1, *(jnp.concatenate([corr_ref[p, j], corr_ref[p, j + 1]], axis=1) for p in (0, 1))
+            )
+            for e in (0, 1):
+                spec_ref[at_re[e], :] = w[:FINE, e * FINE : (e + 1) * FINE]
+                spec_ref[at_im[e], :] = w[FINE:, e * FINE : (e + 1) * FINE]
 
     @pl.when(i >= STEPS)
     def _():
@@ -376,6 +388,7 @@
         out, corr = main_stage(pair.reshape(length, FINE), fspec)
         out = exchange(out.reshape(shards, rows, FINE))
         lags = lax.psum(lags_stage(corr), "chan") * scale
+        lags, _ = lax.optimization_barrier((lags, out))
         lags = merge(exchange(lags.reshape(shards, -1, FINE)).reshape(shards, rows, own))
         return tuple(unpack(out, k_gate, values, grad_out, jnp.asarray(table.T))) + (lags,)
 

time: 344 us -> 280 us (0.81)
  waiting for transfers between devices: 186 us -> 148 us
  Pallas kernels: 102 us -> 85.2 us
  blocking collectives: 14.6 us -> 0 us
    all_to_all x3 -> x4, waiting for transfers between devices: 163 us -> 125 us  [exchange(): return lax.all_to_all(parts, 'seq', split_axis=0, concat_axis=0, tiled=True)]
    pallas_call x3, Pallas kernels: 83 us -> 65.7 us  [stepped(): pl.pallas_call(kernel, grid=(phases * STEPS,), in_specs=in_specs, out_spe...]
    all_to_all x1 -> x0, blocking collectives: 14.6 us -> none  [exchange(): return lax.all_to_all(parts, 'seq', split_axis=0, concat_axis=0, tiled=True)]
    all_to_all x3 -> x4, starting transfers between devices: 19.1 us -> 22.4 us  [exchange(): return lax.all_to_all(parts, 'seq', split_axis=0, concat_axis=0, tiled=True)]
  transfers between devices with their start and end apart: 4 -> 5, of which waited for: 3 -> 3; matrix products, arithmetic and copies ran while one was open for 1% -> 1% of each run, Pallas kernels for 8% -> 20%
where the time goes in v2:
time: 280 us; the launch traced here: 278 us
  waiting for transfers between devices  148 us (53%)
  Pallas kernels  85.2 us (30%)
  starting transfers between devices  22.4 us (8%)
  between operations  14.1 us (5%)
  local copies, waits for them, and re-layouts  5.19 us (2%)
    all_to_all x4, waiting for transfers between devices, exchange(): return lax.all_to_all(parts, 'seq', split_axis=0, concat_axis=0, tiled=True)  125 us
    pallas_call x3, Pallas kernels, stepped(): pl.pallas_call(kernel, grid=(phases * STEPS,), in_specs=in_specs, out_spe...  65.7 us
    psum x1, waiting for transfers between devices, local(): lags = lax.psum(lags_stage(corr), 'chan') * scale  23.8 us
    all_to_all x4, starting transfers between devices, exchange(): return lax.all_to_all(parts, 'seq', split_axis=0, concat_axis=0, tiled=True)  22.4 us
    pallas_call x1, Pallas kernels, pack(): pl.pallas_call(pack_kernel, grid=(rows // tile,), in_specs=[block] * 4 +...  9.75 us
    pallas_call x1, Pallas kernels, unpack(): pl.pallas_call(unpack_kernel, grid=(rows // tile,), in_specs=[pl.BlockSpe...  9.69 us
  transfers between devices with their start and end apart: 5, of which 3 were waited for; matrix products, arithmetic and copies ran while one was open for 1% of the time, Pallas kernels for 20%

profile of v2, /device:TPU:11, one launch (start us, length us, event | category | flops | bytes accessed | tf_op | source)
XLA Modules:
  0.0 277.9 jit_solution(2611981268662387326)
XLA Ops:
  7.2 1.0 broadcast_multiply_fusion.1
  8.1 0.1 copy.23
  8.3 0.8 copy.24
  9.1 1.3 copy.25
  10.4 6.6 %all-to-all-start.1 = ((f32[16,32,128]{2,1,0:T(8,128)}), f32[16,32,128]{2,1,0:T(8,128)S(1)}, u32[]{:S(2)}, u32[]{:S(2)}) async-start(f32[16,32,128]{2,1,0:T(8,128)} %copy.25), calls=%async_computation.1 | async-start | bytes 524288 | tf_op jit(solution)/shard_map/all_to_all | solution.py:380
  17.0 9.8 %pack.1 = f32[16,512,128]{2,1,0:T(8,128)} custom-call(f32[512,1024]{1,0:T(8,128)} %k_ref.3, f32[512,1024]{1,0:T(8,128)} %v_ref.3, f32[512,1024]{1,0:T(8,128)} %o_ref.3, f32[512,1024]{1,0:T(8,128)} %q_ref.1, bf16[1024,1024]{1,0:T(8,128)(2,1)} %constant.16.clone.table_ref), custom_call_target="tpu_custom_call" | custom-call | flops 4294967296 | bytes 12582912 | tf_op jit(solution)/shard_map/pack/pallas_call | solution.py:258
  26.7 0.7 copy-done
  27.4 6.0 %all-to-all-start = ((f32[16,512,128]{2,1,0:T(8,128)}), f32[16,512,128]{2,1,0:T(8,128)}, u32[]{:S(2)}, u32[]{:S(2)}) async-start(f32[16,512,128]{2,1,0:T(8,128)} %pack.1), calls=%async_computation | async-start | bytes 8388608 | tf_op jit(solution)/shard_map/all_to_all | solution.py:380
  33.5 17.0 %filter_spectrum.1.fspec_ref = f32[2,64,128,128]{3,2,1,0:T(8,128)} custom-call(f32[512,128]{1,0:T(8,128)} %bitcast.17, bf16[128,128,192]{2,1,0:T(8,128)(2,1)} %constant.17.clone.first_ref, bf16[2,512,256]{2,1,0:T(8,128)(2,1)} %constant.19.clone.fine_ref, bf16[16,128,128]{2,1,0:T(8,128)(2,1)} %constant.20.clone.spread_ref), custom_call_target="tpu_custom_call" | custom-call | flops 15000000512 | bytes 25165824 | tf_op jit(solution)/shard_map/filter_spectrum/pallas_call | solution.py:307
  50.4 75.5 %all-to-all-done = f32[16,512,128]{2,1,0:T(8,128)} async-done(((f32[16,512,128]{2,1,0:T(8,128)}), f32[16,512,128]{2,1,0:T(8,128)}, u32[]{:S(2)}, u32[]{:S(2)}) %all-to-all-start) | async-done | bytes 4194336 | tf_op jit(solution)/shard_map/all_to_all | solution.py:380
  125.9 30.9 %pair_stage.1 = (f32[8192,128]{1,0:T(8,128)}, f32[2,64,128,128]{3,2,1,0:T(8,128)}) custom-call(f32[8192,128]{1,0:T(8,128)} %bitcast.pair_ref, f32[2,64,128,128]{3,2,1,0:T(8,128)} %filter_spectrum.1.fspec_ref, bf16[128,128,192]{2,1,0:T(8,128)(2,1)} %constant.17.clone.first_ref, bf16[128,64,384]{2,1,0:T(8,128)(2,1)} %constant.18.clone.last_ref, ...), custom_call_target="tpu_custom_call" | custom-call | flops 30000001024 | bytes 25165824 | tf_op jit(solution)/shard_map/pair_stage/pallas_call | solution.py:307
  156.8 4.9 %all-to-all-start.2 = ((f32[16,512,128]{2,1,0:T(8,128)}), f32[16,512,128]{2,1,0:T(8,128)}, u32[]{:S(2)}, u32[]{:S(2)}) async-start(f32[16,512,128]{2,1,0:T(8,128)} %bitcast.14), calls=%async_computation.2 | async-start | bytes 8388608 | tf_op jit(solution)/shard_map/all_to_all | solution.py:380
  161.7 0.0 all-reduce.2.cloned.1.call-start
  161.8 17.9 %lags.1 = f32[512,128]{1,0:T(8,128)} custom-call(f32[2,64,128,128]{3,2,1,0:T(8,128)} %get-tuple-element.14.corr_ref, bf16[128,64,384]{2,1,0:T(8,128)(2,1)} %constant.18.clone.last_ref, bf16[2,512,256]{2,1,0:T(8,128)(2,1)} %constant.19.clone.fine_ref, bf16[16,128,128]{2,1,0:T(8,128)(2,1)} %constant.21.clone.fold_ref), custom_call_target="tpu_custom_call" | custom-call | flops 15000000512 | bytes 25165824 | tf_op jit(solution)/shard_map/lags/pallas_call | solution.py:307
  179.7 0.0 all-reduce.2.cloned.1.call-update
  179.7 23.8 %all-reduce.2.cloned.1.call-done = f32[512,128]{1,0:T(8,128)} async-done(((f32[512,128]{1,0:T(8,128)}), f32[512,128]{1,0:T(8,128)}) %all-reduce.2.cloned.1.call-update) | async-done | bytes 262160 | tf_op jit(solution)/shard_map/psum | solution.py:390
  203.4 1.7 broadcast_multiply_fusion
  205.1 49.1 %all-to-all-done.2.in_ref = f32[16,512,128]{2,1,0:T(8,128)} async-done(((f32[16,512,128]{2,1,0:T(8,128)}), f32[16,512,128]{2,1,0:T(8,128)}, u32[]{:S(2)}, u32[]{:S(2)}) %all-to-all-start.2) | async-done | bytes 4194336 | tf_op jit(solution)/shard_map/all_to_all | solution.py:380
  254.2 4.9 %all-to-all-start.3 = ((f32[16,32,128]{2,1,0:T(8,128)}), f32[16,32,128]{2,1,0:T(8,128)S(1)}, u32[]{:S(2)}, u32[]{:S(2)}) async-start(f32[16,32,128]{2,1,0:T(8,128)} %bitcast.6), calls=%async_computation.3 | async-start | bytes 524288 | tf_op jit(solution)/shard_map/all_to_all | solution.py:380
  259.1 9.7 %unpack.1 = (f32[512,1024]{1,0:T(8,128)}, f32[512,1024]{1,0:T(8,128)}, f32[512,1024]{1,0:T(8,128)}) custom-call(f32[16,512,128]{2,1,0:T(8,128)} %all-to-all-done.2.in_ref, f32[512,1024]{1,0:T(8,128)} %k_ref.3, f32[512,1024]{1,0:T(8,128)} %v_ref.3, f32[512,1024]{1,0:T(8,128)} %o_ref.3, bf16[1024,1024]{1,0:T(8,128)(2,1)} %constant.22.clone.table_ref), custom_call_target="tpu_custom_call" | custom-call | flops 4294967296 | bytes 16777216 | tf_op jit(solution)/shard_map/unpack/pallas_call | solution.py:276
  268.8 0.0 all-to-all-done.3
  268.8 0.6 copy.26
  269.4 0.8 copy.27
  270.2 0.8 copy.28
  (2 shorter events, 0.0 us)
Async XLA Ops:
  10.4 16.3 %all-to-all-start.1 = ((f32[16,32,128]{2,1,0:T(8,128)}), f32[16,32,128]{2,1,0:T(8,128)S(1)}, u32[]{:S(2)}, u32[]{:S(2)}) async-start(f32[16,32,128]{2,1,0:T(8,128)} %copy.25), calls=%async_computation.1 | async-start | bytes 524288 | tf_op jit(solution)/shard_map/all_to_all | solution.py:380
  26.7 0.7 copy-start
  27.4 98.5 %all-to-all-start = ((f32[16,512,128]{2,1,0:T(8,128)}), f32[16,512,128]{2,1,0:T(8,128)}, u32[]{:S(2)}, u32[]{:S(2)}) async-start(f32[16,512,128]{2,1,0:T(8,128)} %pack.1), calls=%async_computation | async-start | bytes 8388608 | tf_op jit(solution)/shard_map/all_to_all | solution.py:380
  156.8 97.4 %all-to-all-start.2 = ((f32[16,512,128]{2,1,0:T(8,128)}), f32[16,512,128]{2,1,0:T(8,128)}, u32[]{:S(2)}, u32[]{:S(2)}) async-start(f32[16,512,128]{2,1,0:T(8,128)} %bitcast.14), calls=%async_computation.2 | async-start | bytes 8388608 | tf_op jit(solution)/shard_map/all_to_all | solution.py:380
  161.7 41.7 %all-reduce.2.cloned.1.call-start = ((), (), s32[]{:S(2)}) async-start(), calls=%async_computation.4 | async-start | bytes 524288 | tf_op jit(solution)/shard_map/psum | solution.py:390
  254.2 14.6 %all-to-all-start.3 = ((f32[16,32,128]{2,1,0:T(8,128)}), f32[16,32,128]{2,1,0:T(8,128)S(1)}, u32[]{:S(2)}, u32[]{:S(2)}) async-start(f32[16,32,128]{2,1,0:T(8,128)} %bitcast.6), calls=%async_computation.3 | async-start | bytes 524288 | tf_op jit(solution)/shard_map/all_to_all | solution.py:380
Sparse Core Ops, SparseCore 0:
  179.8 23.5 all-reduce.1

commit v3 on v2

--- a/solution.py
+++ b/solution.py
@@ -1,3 +1,5 @@
+import functools
+
 import jax
 import jax.numpy as jnp
 import numpy as np
@@ -142,7 +144,7 @@
     return [pl.ds(p, FINE) for p in at]
 
 
-def filter_kernel(filt_ref, first_ref, fine_ref, spread_ref, out_ref, wide_ref, space_ref, spec_ref):
+def filter_kernel(scale, filt_ref, first_ref, fine_ref, spread_ref, out_ref, wide_ref, space_ref, spec_ref):
     i = pl.program_id(0)
     n1 = space_ref.shape[0] // PITCH
     spots = spread_ref.shape[0]
@@ -154,7 +156,7 @@
         short = filt_ref.shape[0]
         for j in range(spots):
             e = spread_ref[j]
-            wide_ref[pl.ds(j, short, stride=spots), :] = dot(high, e) + dot(rest, e)
+            wide_ref[pl.ds(j, short, stride=spots), :] = scale * (dot(high, e) + dot(rest, e))
         for line in range(n1):
             space_ref[line * PITCH : line * PITCH + FINE, :] = wide_ref[line * FINE : (line + 1) * FINE, :]
 
@@ -330,7 +332,7 @@
 
     def filter_stage(filt):
         return stepped(
-            filter_kernel, 2, (filt, first, mats, spread),
+            functools.partial(filter_kernel, float(length) ** -0.5), 2, (filt, first, mats, spread),
             [whole(filt), phase(first, 0, 0), whole(mats), whole(spread)],
             spec, phase(spec, 1, STEPS), [length] + padded, 15_000_000_000, "filter_spectrum",
         )
@@ -350,6 +352,32 @@
         )
 
     return filter_stage, main_stage, lags_stage
+
+
+def place_kernel(*refs):
+    me = lax.axis_index("seq")
+    out_ref = refs[-1]
+    shards = out_ref.shape[0]
+    for hop in range(shards):
+        out_ref[lax.rem(me + shards - hop, shards)] = refs[hop][0]
+
+
+def scatter_around(parts, shards):
+    me = lax.axis_index("seq")
+    came = []
+    for hop in range(shards):
+        part = lax.dynamic_index_in_dim(parts, (me + hop) % shards, 0, keepdims=True)
+        if hop:
+            part = lax.ppermute(part, "seq", [(i, (i + hop) % shards) for i in range(shards)])
+        came.append(part)
+    vmem = pl.BlockSpec(memory_space=pltpu.VMEM)
+    return pl.pallas_call(
+        place_kernel,
+        in_specs=[vmem] * shards,
+        out_specs=vmem,
+        out_shape=jax.ShapeDtypeStruct(parts.shape, parts.dtype),
+        name="place",
+    )(*came)
 
 
 def local(q_gate, k_gate, values, filter_raw, grad_out):
@@ -381,15 +409,18 @@
 
     if 2 * chans == FINE and n1 == 64:
         table = order_table(width, nfilt, own)
-        filt = exchange(split(filter_raw * scale).reshape(shards, -1, FINE))
-        pair = exchange(pack(k_gate, values, grad_out, q_gate, shards, jnp.asarray(table)))
+        filt = exchange(split(filter_raw).reshape(shards, -1, FINE))
+        packed = pack(k_gate, values, grad_out, q_gate, shards, jnp.asarray(table))
+        filt, packed = lax.optimization_barrier((filt, packed))
+        pair = exchange(packed)
         filter_stage, main_stage, lags_stage = spectral(length, own, chans)
         fspec = filter_stage(filt.reshape(-1, FINE))
         out, corr = main_stage(pair.reshape(length, FINE), fspec)
         out = exchange(out.reshape(shards, rows, FINE))
         lags = lax.psum(lags_stage(corr), "chan") * scale
+        lags = scatter_around(lags.reshape(shards, -1, FINE), shards)
         lags, _ = lax.optimization_barrier((lags, out))
-        lags = merge(exchange(lags.reshape(shards, -1, FINE)).reshape(shards, rows, own))
+        lags = merge(lags.reshape(shards, rows, own))
         return tuple(unpack(out, k_gate, values, grad_out, jnp.asarray(table.T))) + (lags,)
 
     def forward(block):

time: 280 us -> 295 us (1.054)
  starting transfers between devices: 22.4 us -> 37.7 us
  waiting for transfers between devices: 148 us -> 144 us
  local copies, waits for them, and re-layouts: 5.19 us -> 8.3 us
    all_to_all x4 -> x3, waiting for transfers between devices: 125 us -> 75.4 us  [exchange(): return lax.all_to_all(parts, 'seq', split_axis=0, concat_axis=0, tiled=True)]
    ppermute x0 -> x15, waiting for transfers between devices: none -> 45 us  [scatter_around(): lax.ppermute(part, 'seq', [(i, (i + hop) % shards) for i in range(shards)])]
    ppermute x0 -> x15, starting transfers between devices: none -> 20 us  [scatter_around(): lax.ppermute(part, 'seq', [(i, (i + hop) % shards) for i in range(shards)])]
    all_to_all x4 -> x3, starting transfers between devices: 22.4 us -> 17.5 us  [exchange(): return lax.all_to_all(parts, 'seq', split_axis=0, concat_axis=0, tiled=True)]
  transfers between devices with their start and end apart: 5 -> 19, of which waited for: 3 -> 7; matrix products, arithmetic and copies ran while one was open for 1% -> 1% of each run, Pallas kernels for 20% -> 16%
where the time goes in v3:
time: 295 us; the launch traced here: 292 us
  waiting for transfers between devices  144 us (49%)
  Pallas kernels  86.9 us (29%)
  starting transfers between devices  37.7 us (13%)
  between operations  14.5 us (5%)
  local copies, waits for them, and re-layouts  8.3 us (3%)
    all_to_all x3, waiting for transfers between devices, exchange(): return lax.all_to_all(parts, 'seq', split_axis=0, concat_axis=0, tiled=True)  75.4 us
    pallas_call x3, Pallas kernels, stepped(): pl.pallas_call(kernel, grid=(phases * STEPS,), in_specs=in_specs, out_spe...  65.9 us
    ppermute x15, waiting for transfers between devices, scatter_around(): lax.ppermute(part, 'seq', [(i, (i + hop) % shards) for i in range(shards)])  45 us
    psum x1, waiting for transfers between devices, local(): lags = lax.psum(lags_stage(corr), 'chan') * scale  23.5 us
    ppermute x15, starting transfers between devices, scatter_around(): lax.ppermute(part, 'seq', [(i, (i + hop) % shards) for i in range(shards)])  20 us
    all_to_all x3, starting transfers between devices, exchange(): return lax.all_to_all(parts, 'seq', split_axis=0, concat_axis=0, tiled=True)  17.5 us
    pallas_call x1, Pallas kernels, pack(): pl.pallas_call(pack_kernel, grid=(rows // tile,), in_specs=[block] * 4 +...  9.76 us
    pallas_call x1, Pallas kernels, unpack(): pl.pallas_call(unpack_kernel, grid=(rows // tile,), in_specs=[pl.BlockSpe...  9.66 us
  transfers between devices with their start and end apart: 19, of which 7 were waited for; matrix products, arithmetic and copies ran while one was open for 1% of the time, Pallas kernels for 16%

profile of v3, /device:TPU:11, one launch (start us, length us, event | category | flops | bytes accessed | tf_op | source)
XLA Modules:
  0.0 292.3 jit_solution(8357588927515253542)
XLA Ops:
  9.1 1.3 copy.26
  10.4 6.6 %all-to-all-start = ((f32[16,32,128]{2,1,0:T(8,128)}), f32[16,32,128]{2,1,0:T(8,128)S(1)}, u32[]{:S(2)}, u32[]{:S(2)}) async-start(f32[16,32,128]{2,1,0:T(8,128)} %copy.26), calls=%async_computation | async-start | bytes 524288 | tf_op jit(solution)/shard_map/all_to_all | solution.py:408
  17.0 9.8 %pack.1 = f32[16,512,128]{2,1,0:T(8,128)} custom-call(f32[512,1024]{1,0:T(8,128)} %k_ref.3, f32[512,1024]{1,0:T(8,128)} %v_ref.3, f32[512,1024]{1,0:T(8,128)} %o_ref.3, f32[512,1024]{1,0:T(8,128)} %q_ref.1, bf16[1024,1024]{1,0:T(8,128)(2,1)} %constant.158.clone.table_ref), custom_call_target="tpu_custom_call" | custom-call | flops 4294967296 | bytes 12582912 | tf_op jit(solution)/shard_map/pack/pallas_call | solution.py:260
  27.4 6.0 %all-to-all-start.1 = ((f32[16,512,128]{2,1,0:T(8,128)}), f32[16,512,128]{2,1,0:T(8,128)}, u32[]{:S(2)}, u32[]{:S(2)}) async-start(f32[16,512,128]{2,1,0:T(8,128)} %pack.1), calls=%async_computation.1 | async-start | bytes 8388608 | tf_op jit(solution)/shard_map/all_to_all | solution.py:408
  33.4 17.0 %filter_spectrum.1.fspec_ref = f32[2,64,128,128]{3,2,1,0:T(8,128)} custom-call(f32[512,128]{1,0:T(8,128)} %bitcast.18, bf16[128,128,192]{2,1,0:T(8,128)(2,1)} %constant.159.clone.first_ref, bf16[2,512,256]{2,1,0:T(8,128)(2,1)} %constant.161.clone.fine_ref, bf16[16,128,128]{2,1,0:T(8,128)(2,1)} %constant.162.clone.spread_ref), custom_call_target="tpu_custom_call" | custom-call | flops 15000000512 | bytes 25165824 | tf_op jit(solution)/shard_map/filter_spectrum/pallas_call | solution.py:309
  50.5 75.4 %all-to-all-done.1 = f32[16,512,128]{2,1,0:T(8,128)} async-done(((f32[16,512,128]{2,1,0:T(8,128)}), f32[16,512,128]{2,1,0:T(8,128)}, u32[]{:S(2)}, u32[]{:S(2)}) %all-to-all-start.1) | async-done | bytes 4194336 | tf_op jit(solution)/shard_map/all_to_all | solution.py:408
  125.9 30.9 %pair_stage.1 = (f32[8192,128]{1,0:T(8,128)}, f32[2,64,128,128]{3,2,1,0:T(8,128)}) custom-call(f32[8192,128]{1,0:T(8,128)} %bitcast.3.pair_ref, f32[2,64,128,128]{3,2,1,0:T(8,128)} %filter_spectrum.1.fspec_ref, bf16[128,128,192]{2,1,0:T(8,128)(2,1)} %constant.159.clone.first_ref, bf16[128,64,384]{2,1,0:T(8,128)(2,1)} %constant.160.clone.last_ref, ...), custom_call_target="tpu_custom_call" | custom-call | flops 30000001024 | bytes 25165824 | tf_op jit(solution)/shard_map/pair_stage/pallas_call | solution.py:309
  156.8 4.9 %all-to-all-start.2 = ((f32[16,512,128]{2,1,0:T(8,128)}), f32[16,512,128]{2,1,0:T(8,128)}, u32[]{:S(2)}, u32[]{:S(2)}) async-start(f32[16,512,128]{2,1,0:T(8,128)} %bitcast.14), calls=%async_computation.2 | async-start | bytes 8388608 | tf_op jit(solution)/shard_map/all_to_all | solution.py:408
  162.0 17.9 %lags.1 = f32[512,128]{1,0:T(8,128)} custom-call(f32[2,64,128,128]{3,2,1,0:T(8,128)} %get-tuple-element.18.corr_ref, bf16[128,64,384]{2,1,0:T(8,128)(2,1)} %constant.160.clone.last_ref, bf16[2,512,256]{2,1,0:T(8,128)(2,1)} %constant.161.clone.fine_ref, bf16[16,128,128]{2,1,0:T(8,128)(2,1)} %constant.163.clone.fold_ref), custom_call_target="tpu_custom_call" | custom-call | flops 15000000512 | bytes 25165824 | tf_op jit(solution)/shard_map/lags/pallas_call | solution.py:309
  180.1 23.5 %all-reduce.2.cloned.1.call-done = f32[512,128]{1,0:T(8,128)} async-done(((f32[512,128]{1,0:T(8,128)}), f32[512,128]{1,0:T(8,128)}) %all-reduce.2.cloned.1.call-update) | async-done | bytes 262160 | tf_op jit(solution)/shard_map/psum | solution.py:420
  205.3 1.9 collective-permute-start
  207.3 1.2 collective-permute-start.1
  209.7 2.9 collective-permute-start.4
  212.5 40.2 %collective-permute-done.refs_1_ = f32[1,32,128]{2,1,0:T(8,128)S(1)} collective-permute-done((f32[1,32,128]{2,1,0:T(8,128)S(1)}, f32[1,32,128]{2,1,0:T(8,128)S(1)}, u32[]{:S(2)}, u32[]{:S(2)}) %collective-permute-start) | collective-permute-done | bytes 16416 | tf_op jit(solution)/shard_map/ppermute | solution.py:371
  253.5 2.9 collective-permute-start.7
  256.4 2.3 collective-permute-start.8
  258.7 2.7 collective-permute-start.9
  262.5 2.0 collective-permute-start.12
  264.5 1.8 collective-permute-start.13
  266.4 1.6 collective-permute-done.13.refs_14_
  268.0 2.4 collective-permute-done.14.refs_15_
  271.0 1.6 place.1
  272.6 1.6 copy.27
  275.8 9.7 %unpack.1 = (f32[512,1024]{1,0:T(8,128)}, f32[512,1024]{1,0:T(8,128)}, f32[512,1024]{1,0:T(8,128)}) custom-call(f32[16,512,128]{2,1,0:T(8,128)} %all-to-all-done.2.in_ref, f32[512,1024]{1,0:T(8,128)} %k_ref.3, f32[512,1024]{1,0:T(8,128)} %v_ref.3, f32[512,1024]{1,0:T(8,128)} %o_ref.3, bf16[1024,1024]{1,0:T(8,128)(2,1)} %constant.164.clone.table_ref), custom_call_target="tpu_custom_call" | custom-call | flops 4294967296 | bytes 16777216 | tf_op jit(solution)/shard_map/unpack/pallas_call | solution.py:278
  (61 shorter events, 9.7 us)
Async XLA Ops:
  10.4 16.3 %all-to-all-start = ((f32[16,32,128]{2,1,0:T(8,128)}), f32[16,32,128]{2,1,0:T(8,128)S(1)}, u32[]{:S(2)}, u32[]{:S(2)}) async-start(f32[16,32,128]{2,1,0:T(8,128)} %copy.26), calls=%async_computation | async-start | bytes 524288 | tf_op jit(solution)/shard_map/all_to_all | solution.py:408
  27.4 98.5 %all-to-all-start.1 = ((f32[16,512,128]{2,1,0:T(8,128)}), f32[16,512,128]{2,1,0:T(8,128)}, u32[]{:S(2)}, u32[]{:S(2)}) async-start(f32[16,512,128]{2,1,0:T(8,128)} %pack.1), calls=%async_computation.1 | async-start | bytes 8388608 | tf_op jit(solution)/shard_map/all_to_all | solution.py:408
  156.8 115.8 %all-to-all-start.2 = ((f32[16,512,128]{2,1,0:T(8,128)}), f32[16,512,128]{2,1,0:T(8,128)}, u32[]{:S(2)}, u32[]{:S(2)}) async-start(f32[16,512,128]{2,1,0:T(8,128)} %bitcast.14), calls=%async_computation.2 | async-start | bytes 8388608 | tf_op jit(solution)/shard_map/all_to_all | solution.py:408
  161.7 41.9 %all-reduce.2.cloned.1.call-start = ((), (), s32[]{:S(2)}) async-start(), calls=%async_computation.3 | async-start | bytes 524288 | tf_op jit(solution)/shard_map/psum | solution.py:420
  205.3 47.5 %collective-permute-start = (f32[1,32,128]{2,1,0:T(8,128)S(1)}, f32[1,32,128]{2,1,0:T(8,128)S(1)}, u32[]{:S(2)}, u32[]{:S(2)}) collective-permute-start(f32[1,32,128]{2,1,0:T(8,128)S(1)} %get-tuple-element.42), channel_id=1, source_target_pairs={{0,2},{2,4},{4,6},{6,8},{8,10},{10,12},{12,14},{14,16},{16,18},{18... | collective-permute-start | bytes 49160 | tf_op jit(solution)/shard_map/ppermute | solution.py:371
  207.3 45.9 %collective-permute-start.1 = (f32[1,32,128]{2,1,0:T(8,128)S(1)}, f32[1,32,128]{2,1,0:T(8,128)S(1)}, u32[]{:S(2)}, u32[]{:S(2)}) collective-permute-start(f32[1,32,128]{2,1,0:T(8,128)S(1)} %get-tuple-element.41), channel_id=1, source_target_pairs={{0,4},{2,6},{4,8},{6,10},{8,12},{10,14},{12,16},{14,18},{16,20},{1... | collective-permute-start | bytes 49160 | tf_op jit(solution)/shard_map/ppermute | solution.py:371
  208.5 45.0 %collective-permute-start.2 = (f32[1,32,128]{2,1,0:T(8,128)S(1)}, f32[1,32,128]{2,1,0:T(8,128)S(1)}, u32[]{:S(2)}, u32[]{:S(2)}) collective-permute-start(f32[1,32,128]{2,1,0:T(8,128)S(1)} %get-tuple-element.40), channel_id=1, source_target_pairs={{0,6},{2,8},{4,10},{6,12},{8,14},{10,16},{12,18},{14,20},{16,22},{... | collective-permute-start | bytes 49160 | tf_op jit(solution)/shard_map/ppermute | solution.py:371
  208.8 47.6 %collective-permute-start.3 = (f32[1,32,128]{2,1,0:T(8,128)S(1)}, f32[1,32,128]{2,1,0:T(8,128)S(1)}, u32[]{:S(2)}, u32[]{:S(2)}) collective-permute-start(f32[1,32,128]{2,1,0:T(8,128)S(1)} %get-tuple-element.39), channel_id=1, source_target_pairs={{0,8},{2,10},{4,12},{6,14},{8,16},{10,18},{12,20},{14,22},{16,24},... | collective-permute-start | bytes 49160 | tf_op jit(solution)/shard_map/ppermute | solution.py:371
  209.7 49.0 %collective-permute-start.4 = (f32[1,32,128]{2,1,0:T(8,128)S(1)}, f32[1,32,128]{2,1,0:T(8,128)S(1)}, u32[]{:S(2)}, u32[]{:S(2)}) collective-permute-start(f32[1,32,128]{2,1,0:T(8,128)S(1)} %get-tuple-element.38), channel_id=1, source_target_pairs={{0,10},{2,12},{4,14},{6,16},{8,18},{10,20},{12,22},{14,24},{16,26}... | collective-permute-start | bytes 49160 | tf_op jit(solution)/shard_map/ppermute | solution.py:371
  252.8 17.6 %copy-start.1 = (f32[1,32,128]{2,1,0:T(8,128)}, f32[1,32,128]{2,1,0:T(8,128)S(1)}, u32[]{:S(2)}) copy-start(f32[1,32,128]{2,1,0:T(8,128)S(1)} %collective-permute-done.refs_1_) | copy-start | bytes 49156
  252.8 8.6 %collective-permute-start.5 = (f32[1,32,128]{2,1,0:T(8,128)S(1)}, f32[1,32,128]{2,1,0:T(8,128)S(1)}, u32[]{:S(2)}, u32[]{:S(2)}) collective-permute-start(f32[1,32,128]{2,1,0:T(8,128)S(1)} %get-tuple-element.37), channel_id=1, source_target_pairs={{0,12},{2,14},{4,16},{6,18},{8,20},{10,22},{12,24},{14,26},{16,28}... | collective-permute-start | bytes 49160 | tf_op jit(solution)/shard_map/ppermute | solution.py:371
  253.1 17.2 %copy-start.2 = (f32[1,32,128]{2,1,0:T(8,128)}, f32[1,32,128]{2,1,0:T(8,128)S(1)}, u32[]{:S(2)}) copy-start(f32[1,32,128]{2,1,0:T(8,128)S(1)} %collective-permute-done.1.refs_2_) | copy-start | bytes 49156
  253.1 8.2 %collective-permute-start.6 = (f32[1,32,128]{2,1,0:T(8,128)S(1)}, f32[1,32,128]{2,1,0:T(8,128)S(1)}, u32[]{:S(2)}, u32[]{:S(2)}) collective-permute-start(f32[1,32,128]{2,1,0:T(8,128)S(1)} %get-tuple-element.36), channel_id=1, source_target_pairs={{0,14},{2,16},{4,18},{6,20},{8,22},{10,24},{12,26},{14,28},{16,30}... | collective-permute-start | bytes 49160 | tf_op jit(solution)/shard_map/ppermute | solution.py:371
  253.5 16.9 %copy-start.3 = (f32[1,32,128]{2,1,0:T(8,128)}, f32[1,32,128]{2,1,0:T(8,128)S(1)}, u32[]{:S(2)}) copy-start(f32[1,32,128]{2,1,0:T(8,128)S(1)} %collective-permute-done.2.refs_3_) | copy-start | bytes 49156
  253.5 9.0 %collective-permute-start.7 = (f32[1,32,128]{2,1,0:T(8,128)S(1)}, f32[1,32,128]{2,1,0:T(8,128)S(1)}, u32[]{:S(2)}, u32[]{:S(2)}) collective-permute-start(f32[1,32,128]{2,1,0:T(8,128)S(1)} %get-tuple-element.35), channel_id=1, source_target_pairs={{0,16},{2,18},{4,20},{6,22},{8,24},{10,26},{12,28},{14,30},{16,0},... | collective-permute-start | bytes 49160 | tf_op jit(solution)/shard_map/ppermute | solution.py:371
  256.4 14.0 %copy-start.4 = (f32[1,32,128]{2,1,0:T(8,128)}, f32[1,32,128]{2,1,0:T(8,128)S(1)}, u32[]{:S(2)}) copy-start(f32[1,32,128]{2,1,0:T(8,128)S(1)} %collective-permute-done.3.refs_4_) | copy-start | bytes 49156
  256.4 8.1 %collective-permute-start.8 = (f32[1,32,128]{2,1,0:T(8,128)S(1)}, f32[1,32,128]{2,1,0:T(8,128)S(1)}, u32[]{:S(2)}, u32[]{:S(2)}) collective-permute-start(f32[1,32,128]{2,1,0:T(8,128)S(1)} %get-tuple-element.34), channel_id=1, source_target_pairs={{0,18},{2,20},{4,22},{6,24},{8,26},{10,28},{12,30},{14,0},{16,2},{... | collective-permute-start | bytes 49160 | tf_op jit(solution)/shard_map/ppermute | solution.py:371
  258.7 11.7 %copy-start.5 = (f32[1,32,128]{2,1,0:T(8,128)}, f32[1,32,128]{2,1,0:T(8,128)S(1)}, u32[]{:S(2)}) copy-start(f32[1,32,128]{2,1,0:T(8,128)S(1)} %collective-permute-done.4.refs_5_) | copy-start | bytes 49156
  258.7 7.6 %collective-permute-start.9 = (f32[1,32,128]{2,1,0:T(8,128)S(1)}, f32[1,32,128]{2,1,0:T(8,128)S(1)}, u32[]{:S(2)}, u32[]{:S(2)}) collective-permute-start(f32[1,32,128]{2,1,0:T(8,128)S(1)} %get-tuple-element.33), channel_id=1, source_target_pairs={{0,20},{2,22},{4,24},{6,26},{8,28},{10,30},{12,0},{14,2},{16,4},{1... | collective-permute-start | bytes 49160 | tf_op jit(solution)/shard_map/ppermute | solution.py:371
  261.4 5.0 %collective-permute-start.10 = (f32[1,32,128]{2,1,0:T(8,128)S(1)}, f32[1,32,128]{2,1,0:T(8,128)S(1)}, u32[]{:S(2)}, u32[]{:S(2)}) collective-permute-start(f32[1,32,128]{2,1,0:T(8,128)S(1)} %get-tuple-element.32), channel_id=1, source_target_pairs={{0,22},{2,24},{4,26},{6,28},{8,30},{10,0},{12,2},{14,4},{16,6},{18... | collective-permute-start | bytes 49160 | tf_op jit(solution)/shard_map/ppermute | solution.py:371
  261.4 4.9 %collective-permute-start.11 = (f32[1,32,128]{2,1,0:T(8,128)S(1)}, f32[1,32,128]{2,1,0:T(8,128)S(1)}, u32[]{:S(2)}, u32[]{:S(2)}) collective-permute-start(f32[1,32,128]{2,1,0:T(8,128)S(1)} %get-tuple-element.31), channel_id=1, source_target_pairs={{0,24},{2,26},{4,28},{6,30},{8,0},{10,2},{12,4},{14,6},{16,8},{18,... | collective-permute-start | bytes 49160 | tf_op jit(solution)/shard_map/ppermute | solution.py:371
  262.5 3.8 %collective-permute-start.12 = (f32[1,32,128]{2,1,0:T(8,128)S(1)}, f32[1,32,128]{2,1,0:T(8,128)S(1)}, u32[]{:S(2)}, u32[]{:S(2)}) collective-permute-start(f32[1,32,128]{2,1,0:T(8,128)S(1)} %get-tuple-element.30), channel_id=1, source_target_pairs={{0,26},{2,28},{4,30},{6,0},{8,2},{10,4},{12,6},{14,8},{16,10},{18,... | collective-permute-start | bytes 49160 | tf_op jit(solution)/shard_map/ppermute | solution.py:371
  264.5 3.5 %collective-permute-start.13 = (f32[1,32,128]{2,1,0:T(8,128)S(1)}, f32[1,32,128]{2,1,0:T(8,128)S(1)}, u32[]{:S(2)}, u32[]{:S(2)}) collective-permute-start(f32[1,32,128]{2,1,0:T(8,128)S(1)} %get-tuple-element.29), channel_id=1, source_target_pairs={{0,28},{2,30},{4,0},{6,2},{8,4},{10,6},{12,8},{14,10},{16,12},{18,... | collective-permute-start | bytes 49160 | tf_op jit(solution)/shard_map/ppermute | solution.py:371
  266.3 4.1 %collective-permute-start.14 = (f32[1,32,128]{2,1,0:T(8,128)S(1)}, f32[1,32,128]{2,1,0:T(8,128)S(1)}, u32[]{:S(2)}, u32[]{:S(2)}) collective-permute-start(f32[1,32,128]{2,1,0:T(8,128)S(1)} %get-tuple-element.28), channel_id=1, source_target_pairs={{0,30},{2,0},{4,2},{6,4},{8,6},{10,8},{12,10},{14,12},{16,14},{18,... | collective-permute-start | bytes 49160 | tf_op jit(solution)/shard_map/ppermute | solution.py:371
  (11 other events, 52.2 us)
Sparse Core Ops, SparseCore 0:
  180.0 23.5 all-reduce.1

commit v4 on v2

--- a/solution.py
+++ b/solution.py
@@ -1,3 +1,5 @@
+import functools
+
 import jax
 import jax.numpy as jnp
 import numpy as np
@@ -142,7 +144,7 @@
     return [pl.ds(p, FINE) for p in at]
 
 
-def filter_kernel(filt_ref, first_ref, fine_ref, spread_ref, out_ref, wide_ref, space_ref, spec_ref):
+def filter_kernel(scale, filt_ref, first_ref, fine_ref, spread_ref, out_ref, wide_ref, space_ref, spec_ref):
     i = pl.program_id(0)
     n1 = space_ref.shape[0] // PITCH
     spots = spread_ref.shape[0]
@@ -154,7 +156,7 @@
         short = filt_ref.shape[0]
         for j in range(spots):
             e = spread_ref[j]
-            wide_ref[pl.ds(j, short, stride=spots), :] = dot(high, e) + dot(rest, e)
+            wide_ref[pl.ds(j, short, stride=spots), :] = scale * (dot(high, e) + dot(rest, e))
         for line in range(n1):
             space_ref[line * PITCH : line * PITCH + FINE, :] = wide_ref[line * FINE : (line + 1) * FINE, :]
 
@@ -330,7 +332,7 @@
 
     def filter_stage(filt):
         return stepped(
-            filter_kernel, 2, (filt, first, mats, spread),
+            functools.partial(filter_kernel, float(length) ** -0.5), 2, (filt, first, mats, spread),
             [whole(filt), phase(first, 0, 0), whole(mats), whole(spread)],
             spec, phase(spec, 1, STEPS), [length] + padded, 15_000_000_000, "filter_spectrum",
         )
@@ -381,16 +383,19 @@
 
     if 2 * chans == FINE and n1 == 64:
         table = order_table(width, nfilt, own)
-        filt = exchange(split(filter_raw * scale).reshape(shards, -1, FINE))
-        pair = exchange(pack(k_gate, values, grad_out, q_gate, shards, jnp.asarray(table)))
+        filt = exchange(split(filter_raw).reshape(shards, -1, FINE))
+        packed = pack(k_gate, values, grad_out, q_gate, shards, jnp.asarray(table))
+        filt, packed = lax.optimization_barrier((filt, packed))
+        pair = exchange(packed)
         filter_stage, main_stage, lags_stage = spectral(length, own, chans)
         fspec = filter_stage(filt.reshape(-1, FINE))
         out, corr = main_stage(pair.reshape(length, FINE), fspec)
         out = exchange(out.reshape(shards, rows, FINE))
         lags = lax.psum(lags_stage(corr), "chan") * scale
-        lags, _ = lax.optimization_barrier((lags, out))
+        grads = unpack(out, k_gate, values, grad_out, jnp.asarray(table.T))
+        lags, _ = lax.optimization_barrier((lags, grads[0]))
         lags = merge(exchange(lags.reshape(shards, -1, FINE)).reshape(shards, rows, own))
-        return tuple(unpack(out, k_gate, values, grad_out, jnp.asarray(table.T))) + (lags,)
+        return tuple(grads) + (lags,)
 
     def forward(block):
         wide = block.shape[1]

time: 280 us -> 290 us (1.036)
  blocking collectives: 0 us -> 12.6 us
  starting transfers between devices: 22.4 us -> 17.7 us
    all_to_all x0 -> x1, blocking collectives: none -> 12.6 us  [exchange(): return lax.all_to_all(parts, 'seq', split_axis=0, concat_axis=0, tiled=True)]
    all_to_all x4 -> x3, starting transfers between devices: 22.4 us -> 17.5 us  [exchange(): return lax.all_to_all(parts, 'seq', split_axis=0, concat_axis=0, tiled=True)]
    all_to_all x4 -> x3, waiting for transfers between devices: 125 us -> 125 us  [exchange(): return lax.all_to_all(parts, 'seq', split_axis=0, concat_axis=0, tiled=True)]
  transfers between devices with their start and end apart: 5 -> 4, of which waited for: 3 -> 3; matrix products, arithmetic and copies ran while one was open for 1% -> 0% of each run, Pallas kernels for 20% -> 16%
where the time goes in v4:
time: 290 us; the launch traced here: 286 us
  waiting for transfers between devices  149 us (51%)
  Pallas kernels  85.2 us (29%)
  starting transfers between devices  17.7 us (6%)
  between operations  14.1 us (5%)
  blocking collectives  12.6 us (4%)
  local copies, waits for them, and re-layouts  6.13 us (2%)
    all_to_all x3, waiting for transfers between devices, exchange(): return lax.all_to_all(parts, 'seq', split_axis=0, concat_axis=0, tiled=True)  125 us
    pallas_call x3, Pallas kernels, stepped(): pl.pallas_call(kernel, grid=(phases * STEPS,), in_specs=in_specs, out_spe...  65.8 us
    psum x1, waiting for transfers between devices, local(): lags = lax.psum(lags_stage(corr), 'chan') * scale  23.8 us
    all_to_all x3, starting transfers between devices, exchange(): return lax.all_to_all(parts, 'seq', split_axis=0, concat_axis=0, tiled=True)  17.5 us
    all_to_all x1, blocking collectives, exchange(): return lax.all_to_all(parts, 'seq', split_axis=0, concat_axis=0, tiled=True)  12.6 us
    pallas_call x1, Pallas kernels, pack(): pl.pallas_call(pack_kernel, grid=(rows // tile,), in_specs=[block] * 4 +...  9.75 us
    pallas_call x1, Pallas kernels, unpack(): pl.pallas_call(unpack_kernel, grid=(rows // tile,), in_specs=[pl.BlockSpe...  9.66 us
  transfers between devices with their start and end apart: 4, of which 3 were waited for; matrix products, arithmetic and copies ran while one was open for 0% of the time, Pallas kernels for 16%

profile of v4, /device:TPU:11, one launch (start us, length us, event | category | flops | bytes accessed | tf_op | source)
XLA Modules:
  0.0 285.6 jit_solution(4840892901292711291)
XLA Ops:
  7.2 1.1 copy.24
  8.2 0.8 copy.25
  9.1 1.3 copy.26
  10.4 6.6 %all-to-all-start = ((f32[16,32,128]{2,1,0:T(8,128)}), f32[16,32,128]{2,1,0:T(8,128)S(1)}, u32[]{:S(2)}, u32[]{:S(2)}) async-start(f32[16,32,128]{2,1,0:T(8,128)} %copy.26), calls=%async_computation | async-start | bytes 524288 | tf_op jit(solution)/shard_map/all_to_all | solution.py:382
  17.0 9.8 %pack.1 = f32[16,512,128]{2,1,0:T(8,128)} custom-call(f32[512,1024]{1,0:T(8,128)} %k_ref.3, f32[512,1024]{1,0:T(8,128)} %v_ref.3, f32[512,1024]{1,0:T(8,128)} %o_ref.3, f32[512,1024]{1,0:T(8,128)} %q_ref.1, bf16[1024,1024]{1,0:T(8,128)(2,1)} %constant.16.clone.table_ref), custom_call_target="tpu_custom_call" | custom-call | flops 4294967296 | bytes 12582912 | tf_op jit(solution)/shard_map/pack/pallas_call | solution.py:260
  26.7 0.0 all-to-all-done
  26.7 0.0 copy-start
  26.7 0.7 copy-done
  27.4 6.0 %all-to-all-start.1 = ((f32[16,512,128]{2,1,0:T(8,128)}), f32[16,512,128]{2,1,0:T(8,128)}, u32[]{:S(2)}, u32[]{:S(2)}) async-start(f32[16,512,128]{2,1,0:T(8,128)} %pack.1), calls=%async_computation.1 | async-start | bytes 8388608 | tf_op jit(solution)/shard_map/all_to_all | solution.py:382
  33.4 17.0 %filter_spectrum.1.fspec_ref = f32[2,64,128,128]{3,2,1,0:T(8,128)} custom-call(f32[512,128]{1,0:T(8,128)} %bitcast.18, bf16[128,128,192]{2,1,0:T(8,128)(2,1)} %constant.17.clone.first_ref, bf16[2,512,256]{2,1,0:T(8,128)(2,1)} %constant.19.clone.fine_ref, bf16[16,128,128]{2,1,0:T(8,128)(2,1)} %constant.20.clone.spread_ref), custom_call_target="tpu_custom_call" | custom-call | flops 15000000512 | bytes 25165824 | tf_op jit(solution)/shard_map/filter_spectrum/pallas_call | solution.py:309
  50.4 75.5 %all-to-all-done.1 = f32[16,512,128]{2,1,0:T(8,128)} async-done(((f32[16,512,128]{2,1,0:T(8,128)}), f32[16,512,128]{2,1,0:T(8,128)}, u32[]{:S(2)}, u32[]{:S(2)}) %all-to-all-start.1) | async-done | bytes 4194336 | tf_op jit(solution)/shard_map/all_to_all | solution.py:382
  125.9 30.9 %pair_stage.1 = (f32[8192,128]{1,0:T(8,128)}, f32[2,64,128,128]{3,2,1,0:T(8,128)}) custom-call(f32[8192,128]{1,0:T(8,128)} %bitcast.3.pair_ref, f32[2,64,128,128]{3,2,1,0:T(8,128)} %filter_spectrum.1.fspec_ref, bf16[128,128,192]{2,1,0:T(8,128)(2,1)} %constant.17.clone.first_ref, bf16[128,64,384]{2,1,0:T(8,128)(2,1)} %constant.18.clone.last_ref, ...), custom_call_target="tpu_custom_call" | custom-call | flops 30000001024 | bytes 25165824 | tf_op jit(solution)/shard_map/pair_stage/pallas_call | solution.py:309
  156.8 4.9 %all-to-all-start.2 = ((f32[16,512,128]{2,1,0:T(8,128)}), f32[16,512,128]{2,1,0:T(8,128)}, u32[]{:S(2)}, u32[]{:S(2)}) async-start(f32[16,512,128]{2,1,0:T(8,128)} %bitcast.14), calls=%async_computation.2 | async-start | bytes 8388608 | tf_op jit(solution)/shard_map/all_to_all | solution.py:382
  161.7 0.2 all-reduce.2.cloned.1.call-start
  161.9 17.9 %lags.1 = f32[512,128]{1,0:T(8,128)} custom-call(f32[2,64,128,128]{3,2,1,0:T(8,128)} %get-tuple-element.18.corr_ref, bf16[128,64,384]{2,1,0:T(8,128)(2,1)} %constant.18.clone.last_ref, bf16[2,512,256]{2,1,0:T(8,128)(2,1)} %constant.19.clone.fine_ref, bf16[16,128,128]{2,1,0:T(8,128)(2,1)} %constant.21.clone.fold_ref), custom_call_target="tpu_custom_call" | custom-call | flops 15000000512 | bytes 25165824 | tf_op jit(solution)/shard_map/lags/pallas_call | solution.py:309
  179.8 0.0 all-reduce.2.cloned.1.call-update
  179.9 23.8 %all-reduce.2.cloned.1.call-done = f32[512,128]{1,0:T(8,128)} async-done(((f32[512,128]{1,0:T(8,128)}), f32[512,128]{1,0:T(8,128)}) %all-reduce.2.cloned.1.call-update) | async-done | bytes 262160 | tf_op jit(solution)/shard_map/psum | solution.py:394
  203.6 1.0 broadcast_multiply_fusion
  204.6 49.6 %all-to-all-done.2.in_ref = f32[16,512,128]{2,1,0:T(8,128)} async-done(((f32[16,512,128]{2,1,0:T(8,128)}), f32[16,512,128]{2,1,0:T(8,128)}, u32[]{:S(2)}, u32[]{:S(2)}) %all-to-all-start.2) | async-done | bytes 4194336 | tf_op jit(solution)/shard_map/all_to_all | solution.py:382
  254.2 9.7 %unpack.1 = (f32[512,1024]{1,0:T(8,128)}, f32[512,1024]{1,0:T(8,128)}, f32[512,1024]{1,0:T(8,128)}) custom-call(f32[16,512,128]{2,1,0:T(8,128)} %all-to-all-done.2.in_ref, f32[512,1024]{1,0:T(8,128)} %k_ref.3, f32[512,1024]{1,0:T(8,128)} %v_ref.3, f32[512,1024]{1,0:T(8,128)} %o_ref.3, bf16[1024,1024]{1,0:T(8,128)(2,1)} %constant.22.clone.table_ref), custom_call_target="tpu_custom_call" | custom-call | flops 4294967296 | bytes 16777216 | tf_op jit(solution)/shard_map/unpack/pallas_call | solution.py:278
  263.8 12.6 %all_to_all.20 = f32[16,32,128]{2,1,0:T(8,128)S(1)} all-to-all(f32[16,32,128]{2,1,0:T(8,128)S(1)} %bitcast.17), channel_id=1, replica_groups=mesh['seq'=16,'chan'=2] {'seq'}, dimensions={0} | all-to-all | bytes 524288 | tf_op jit(solution)/shard_map/all_to_all | solution.py:382
  276.5 0.6 copy.27
  277.1 0.8 copy.28
  277.9 0.8 copy.29
Async XLA Ops:
  10.4 16.3 %all-to-all-start = ((f32[16,32,128]{2,1,0:T(8,128)}), f32[16,32,128]{2,1,0:T(8,128)S(1)}, u32[]{:S(2)}, u32[]{:S(2)}) async-start(f32[16,32,128]{2,1,0:T(8,128)} %copy.26), calls=%async_computation | async-start | bytes 524288 | tf_op jit(solution)/shard_map/all_to_all | solution.py:382
  26.7 0.7 copy-start
  27.4 98.5 %all-to-all-start.1 = ((f32[16,512,128]{2,1,0:T(8,128)}), f32[16,512,128]{2,1,0:T(8,128)}, u32[]{:S(2)}, u32[]{:S(2)}) async-start(f32[16,512,128]{2,1,0:T(8,128)} %pack.1), calls=%async_computation.1 | async-start | bytes 8388608 | tf_op jit(solution)/shard_map/all_to_all | solution.py:382
  156.8 97.4 %all-to-all-start.2 = ((f32[16,512,128]{2,1,0:T(8,128)}), f32[16,512,128]{2,1,0:T(8,128)}, u32[]{:S(2)}, u32[]{:S(2)}) async-start(f32[16,512,128]{2,1,0:T(8,128)} %bitcast.14), calls=%async_computation.2 | async-start | bytes 8388608 | tf_op jit(solution)/shard_map/all_to_all | solution.py:382
  161.7 41.9 %all-reduce.2.cloned.1.call-start = ((), (), s32[]{:S(2)}) async-start(), calls=%async_computation.4 | async-start | bytes 524288 | tf_op jit(solution)/shard_map/psum | solution.py:394
Sparse Core Ops, SparseCore 0:
  180.0 23.5 all-reduce.1
